TPU v7x, 512 devices: a whole 4x8x8 slice. The times are simulated.
512 devices in a mesh: node: 32 (over x, z), feat: 16 (over y, core).
Axes of the slice: x: 4, y: 8, z: 8, core: 2. Of those that a mesh axis runs over, the one named last changes fastest.
Arguments:
- x_far: bfloat16 [128, 524288], P('feat', 'node'), may hold values from -6 to 6
- x_near: bfloat16 [128, 65536], P('feat', 'node'), may hold values from -6 to 6
- tile_src: int32 [32768], P('node'), may hold values from 0 to 127
- tile_dst: int32 [32768], P('node'), may hold values from 0 to 15
- tile_rows: int32 [32768], P('node'), may hold values from 0 to 128, as said below
- tile_cols: int32 [32768, 4, 128], P('node'), may hold values from 0 to 127
- seed_nbrs: int32 [4096, 10], P('node'), may hold values from 0 to 2047
- labels: int32 [4096], P('node'), may hold values from 0 to 171
- self_one: bfloat16 [256, 128], P(None, 'feat'), may hold values from -0.5 to 0.5
- neigh_one: bfloat16 [256, 128], P(None, 'feat'), may hold values from -0.5 to 0.5
- self_two: bfloat16 [172, 256], P(None, 'feat'), may hold values from -0.375 to 0.375
- neigh_two: bfloat16 [172, 256], P(None, 'feat'), may hold values from -0.375 to 0.375
Outputs:
- logits: float32 [172, 4096], P(None, 'node')
- loss: float32 [4096], P('node')
Inputs may be any that keep to these rules, and one draw needn't show every extreme that they name: `tile_rows`: slots j with (j mod 32) < a count are used; for some target devices every source device fills all 32 slots; slot 0 of every source and target pair holds 128 rows.
All inputs are finite; a program needn't handle non-finite values.
Results may differ from a plain program's by a relative error of at most 0.003.
Values may be sent and summed in bfloat16 or wider, within the bound.
A program may use at most 64 MiB of HBM per device.

v0:
```python
import jax
import jax.numpy as jnp
from jax import lax
from jax.sharding import PartitionSpec as P

FAN2 = 10


def tile_counts(cols, rows):
    lanes = jnp.arange(128, dtype=jnp.int32)
    live = (lanes[None, :] < rows[:, None]).astype(jnp.float32)
    hits = jnp.sum((cols[..., None] == lanes).astype(jnp.bfloat16), axis=1)
    return (hits * live[:, :, None].astype(jnp.bfloat16), live)


def per_device(
    x_far,
    x_near,
    tile_src,
    tile_dst,
    tile_rows,
    tile_cols,
    seed_nbrs,
    labels,
    self_one,
    neigh_one,
    self_two,
    neigh_two,
):
    nodes = lax.axis_size("node")
    feats = x_far.shape[0]
    near_count = x_near.shape[1]
    nb1 = near_count // 128
    slots = tile_src.shape[0] // nodes
    depth = tile_cols.shape[1]
    seeds = labels.shape[0]
    blocks = x_far.reshape(feats, x_far.shape[1] // 128, 128)

    def group(parts):
        src_g, cols_g, rows_g = parts
        counts, live = tile_counts(cols_g, rows_g)
        chosen = jnp.take(blocks, src_g, axis=1)
        return (
            jnp.einsum("fgc,grc->gfr", chosen, counts, preferred_element_type=jnp.float32),
            live,
        )

    partial_value, live = lax.map(
        group,
        (
            tile_src.reshape(nodes, slots),
            tile_cols.reshape(nodes, slots, depth, 128),
            tile_rows.reshape(nodes, slots),
        ),
    )
    targets = tile_dst.reshape(nodes, slots)
    block_ids = jnp.arange(nb1, dtype=jnp.int32)
    got, got_dst, got_rows = (
        lax.all_to_all(partial_value, "node", split_axis=0, concat_axis=0, tiled=True),
        lax.all_to_all(targets, "node", split_axis=0, concat_axis=0, tiled=True),
        lax.all_to_all(
            tile_rows.reshape(nodes, slots), "node", split_axis=0, concat_axis=0, tiled=True
        ),
    )
    select = (block_ids[:, None] == got_dst.reshape(-1)[None, :]).astype(jnp.float32)
    lanes = jnp.arange(128, dtype=jnp.int32)
    weight = depth * (lanes[None, :] < got_rows.reshape(-1)[:, None]).astype(jnp.float32)
    agg = jnp.einsum(
        "br,rfc->fbc", select, got.reshape(-1, feats, 128), precision=lax.Precision.HIGHEST
    )
    deg = jnp.dot(select, weight, precision=lax.Precision.HIGHEST)
    agg = agg.reshape(feats, near_count)
    deg = deg.reshape(near_count)
    mean_one = (agg / jnp.maximum(deg, 1.0)[None, :]).astype(jnp.bfloat16)
    node_ids = jnp.arange(near_count, dtype=jnp.int32)
    counts_two = jnp.sum((node_ids[:, None, None] == seed_nbrs[None]).astype(jnp.bfloat16), axis=2)
    z_part = jnp.dot(self_one, x_near, preferred_element_type=jnp.float32) + jnp.dot(
        neigh_one, mean_one, preferred_element_type=jnp.float32
    )
    z_share = lax.psum_scatter(z_part, "feat", scatter_dimension=0, tiled=True)
    hidden = jnp.maximum(z_share, 0.0).astype(jnp.bfloat16)
    mean_two = (jnp.dot(hidden, counts_two, preferred_element_type=jnp.float32) / FAN2).astype(
        jnp.bfloat16
    )
    part_logits = jnp.dot(
        self_two, hidden[:, :seeds], preferred_element_type=jnp.float32
    ) + jnp.dot(neigh_two, mean_two, preferred_element_type=jnp.float32)
    logits = lax.psum(part_logits, "feat")
    classes = jnp.arange(logits.shape[0], dtype=jnp.int32)
    total = jnp.log(jnp.sum(jnp.exp(logits), axis=0))
    picked = jnp.sum(jnp.where(classes[:, None] == labels[None, :], logits, 0.0), axis=0)
    return (logits, total - picked)


def solution(mesh):
    placed = (
        P("feat", "node"),
        P("feat", "node"),
        P("node"),
        P("node"),
        P("node"),
        P("node", None, None),
        P("node", None),
        P("node"),
        P(None, "feat"),
        P(None, "feat"),
        P(None, "feat"),
        P(None, "feat"),
    )
    return jax.shard_map(
        per_device,
        mesh=mesh,
        in_specs=placed,
        out_specs=(P(None, "node"), P("node")),
        check_vma=False,
    )
```

profile of v0, /device:TPU:1, one launch (start us, length us, event | category | flops | bytes accessed | tf_op | source)
XLA Modules:
  0.0 552.5 jit_solution(2987447347520451342)
XLA Ops:
  8.6 13.7 %all-to-all-start.1 = ((s32[32,1,32]{2,1,0:T(1,128)}), s32[32,1,32]{2,1,0:T(1,128)S(1)}, u32[]{:S(2)}, u32[]{:S(2)}) async-start(s32[32,1,32]{2,1,0:T(1,128)} %all_to_all.16), calls=%async_computation.1 | async-start | bytes 32768 | tf_op jit(solution)/shard_map/all_to_all | solution.py:60
  25.2 5.7 %all-to-all-done.1 = s32[32,1,32]{2,1,0:T(1,128)S(1)} async-done(((s32[32,1,32]{2,1,0:T(1,128)}), s32[32,1,32]{2,1,0:T(1,128)S(1)}, u32[]{:S(2)}, u32[]{:S(2)}) %all-to-all-start.1) | async-done | bytes 4128 | tf_op jit(solution)/shard_map/all_to_all | solution.py:60
  30.8 3.8 all-to-all-start.2
  34.6 226.8 %while.12 = (s32[]{:T(128)}, f32[32,32,8,128]{3,2,1,0:T(8,128)}, s32[32,32]{1,0:T(8,128)S(1)}, bf16[8,128,128]{2,0,1:T(8,128)(2,1)}, s32[32,32,4,128]{3,2,1,0:T(4,128)}, /*index=5*/s32[32,32]{1,0:T(8,128)S(1)}, s32[]{:T(128)}) while((s32[]{:T(128)}, f32[32,32,8,128]{3,2,1,0:T(8,128)}, s32[32,32]{1,0:T(8,128)S(1)}, ...), condition=%wide.region_2.3_spmd, body=%wide.region_0.2_spmd.sunk | while | flops 14726434 | bytes 2643613 | solution.py:48
  37.1 3.0 fusion.52
  44.2 3.0 fusion.52
  51.3 3.0 fusion.52
  58.4 3.0 fusion.52
  65.4 3.0 fusion.52
  72.5 3.0 fusion.52
  79.6 3.0 fusion.52
  86.7 3.0 fusion.52
  93.8 3.0 fusion.52
  100.9 3.0 fusion.52
  108.0 3.0 fusion.52
  115.1 3.0 fusion.52
  122.1 3.0 fusion.52
  129.2 3.0 fusion.52
  136.3 3.0 fusion.52
  143.4 3.0 fusion.52
  150.5 3.0 fusion.52
  157.6 3.0 fusion.52
  164.7 3.0 fusion.52
  171.8 3.0 fusion.52
  178.8 3.0 fusion.52
  185.9 3.0 fusion.52
  193.0 3.0 fusion.52
  261.4 9.5 %all-to-all-start = ((f32[32,32,8,128]{3,2,1,0:T(8,128)}), f32[32,32,8,128]{3,2,1,0:T(8,128)}, u32[]{:S(2)}, u32[]{:S(2)}) async-start(f32[32,32,8,128]{3,2,1,0:T(8,128)} %get-tuple-element.79), calls=%async_computation | async-start | bytes 8388608 | tf_op jit(solution)/shard_map/all_to_all | solution.py:59
  273.9 89.5 %all-to-all-done = f32[32,32,8,128]{3,2,1,0:T(8,128)} async-done(((f32[32,32,8,128]{3,2,1,0:T(8,128)}), f32[32,32,8,128]{3,2,1,0:T(8,128)}, u32[]{:S(2)}, u32[]{:S(2)}) %all-to-all-start) | async-done | bytes 4194336 | tf_op jit(solution)/shard_map/all_to_all | solution.py:59
  363.4 3.0 copy.21
  371.1 59.2 %reduce-scatter.2.cloned.1.call-done = f32[16,2048]{1,0:T(8,128)} async-done(((f32[256,2048]{1,0:T(8,128)}), f32[16,2048]{1,0:T(8,128)}) %reduce-scatter.2.cloned.1.call-update) | async-done | bytes 131088 | tf_op jit(solution)/shard_map/reduce_scatter | solution.py:80
  432.4 110.3 %all-reduce.2.cloned.1.call-done = f32[172,128]{1,0:T(8,128)} async-done(((f32[172,128]{1,0:T(8,128)}), f32[172,128]{1,0:T(8,128)}) %all-reduce.2.cloned.1.call-update) | async-done | bytes 88080 | tf_op jit(solution)/shard_map/psum | solution.py:88
  (305 shorter events, 174.3 us)
Async XLA Ops:
  7.2 263.8 %copy-start = (bf16[8,2048]{1,0:T(8,128)(2,1)S(1)}, bf16[8,2048]{1,0:T(8,128)(2,1)}, u32[]{:S(2)}) copy-start(bf16[8,2048]{1,0:T(8,128)(2,1)} %param.15) | copy-start | bytes 98308
  8.6 22.3 %all-to-all-start.1 = ((s32[32,1,32]{2,1,0:T(1,128)}), s32[32,1,32]{2,1,0:T(1,128)S(1)}, u32[]{:S(2)}, u32[]{:S(2)}) async-start(s32[32,1,32]{2,1,0:T(1,128)} %all_to_all.16), calls=%async_computation.1 | async-start | bytes 32768 | tf_op jit(solution)/shard_map/all_to_all | solution.py:60
  30.8 230.6 %all-to-all-start.2 = ((s32[32,1,32]{2,1,0:T(1,128)}), s32[32,1,32]{2,1,0:T(1,128)S(1)}, u32[]{:S(2)}, u32[]{:S(2)}) async-start(s32[32,1,32]{2,1,0:T(1,128)} %all_to_all.18), calls=%async_computation.2 | async-start | bytes 32768 | tf_op jit(solution)/shard_map/all_to_all | solution.py:61
  261.4 9.6 %copy-start.4 = (bf16[256,8]{0,1:T(8,128)(2,1)S(1)}, bf16[256,8]{0,1:T(8,128)(2,1)}, u32[]{:S(2)}) copy-start(bf16[256,8]{0,1:T(8,128)(2,1)} %param.22) | copy-start | bytes 12292
  261.4 101.9 %all-to-all-start = ((f32[32,32,8,128]{3,2,1,0:T(8,128)}), f32[32,32,8,128]{3,2,1,0:T(8,128)}, u32[]{:S(2)}, u32[]{:S(2)}) async-start(f32[32,32,8,128]{3,2,1,0:T(8,128)} %get-tuple-element.79), calls=%async_computation | async-start | bytes 8388608 | tf_op jit(solution)/shard_map/all_to_all | solution.py:59
  270.9 159.3 %reduce-scatter.2.cloned.1.call-start = ((), (), s32[]{:S(2)}) async-start(), calls=%async_computation.4 | async-start | bytes 2228224 | tf_op jit(solution)/shard_map/reduce_scatter | solution.py:80
  366.4 1.5 copy-start.5
  367.9 2.0 copy-start.1
  367.9 63.3 %copy-start.3 = (bf16[172,16]{0,1:T(8,128)(2,1)S(1)}, bf16[172,16]{0,1:T(8,128)(2,1)}, u32[]{:S(2)}) copy-start(bf16[172,16]{0,1:T(8,128)(2,1)} %param.24) | copy-start | bytes 16516
  367.9 63.5 %copy-start.2 = (bf16[172,16]{0,1:T(8,128)(2,1)S(1)}, bf16[172,16]{0,1:T(8,128)(2,1)}, u32[]{:S(2)}) copy-start(bf16[172,16]{0,1:T(8,128)(2,1)} %param.25) | copy-start | bytes 16516
  367.9 174.7 %copy-start.6 = (s32[128]{0:T(128)S(1)}, s32[128]{0:T(128)}, u32[]{:S(2)}) copy-start(s32[128]{0:T(128)} %param.21) | copy-start | bytes 1540
  369.8 172.9 %all-reduce.2.cloned.1.call-start = ((), (), s32[]{:S(2)}) async-start(), calls=%async_computation.5 | async-start | bytes 180224 | tf_op jit(solution)/shard_map/psum | solution.py:88
Sparse Core Ops, SparseCore 0:
  369.9 60.2 reduce-scatter.1
  433.2 109.4 all-reduce.1
where the time goes:
time: 556 us; the launch traced here: 553 us
  waiting for transfers between devices  265 us (48%)
  other arithmetic  104 us (19%)
  local copies, waits for them, and re-layouts  86.5 us (16%)
  matrix products  55.5 us (10%)
  starting transfers between devices  27.1 us (5%)
  between operations  14.2 us (3%)
    psum x1, waiting for transfers between devices, per_device(): logits = lax.psum(part_logits, 'feat')  110 us
    reduce_sum x32, other arithmetic, tile_counts(): hits = jnp.sum((cols[..., None] == lanes).astype(jnp.bfloat16), axis=1)  95.5 us
    all_to_all x1, waiting for transfers between devices, per_device(): lax.all_to_all(partial_value, 'node', split_axis=0, concat_axis=0, tiled=...  89.5 us
    reduce_scatter x1, waiting for transfers between devices, per_device(): z_share = lax.psum_scatter(z_part, 'feat', scatter_dimension=0, tiled=True)  59.2 us
    dot_general x32, matrix products, group(): jnp.einsum('fgc,grc->gfr', chosen, counts, preferred_element_type=jnp.flo...  50.1 us
    gather x32, local copies, waits for them, and re-layouts, group(): chosen = jnp.take(blocks, src_g, axis=1)  49.4 us
    eq x32, local copies, waits for them, and re-layouts, tile_counts(): hits = jnp.sum((cols[..., None] == lanes).astype(jnp.bfloat16), axis=1)  27.2 us
    all_to_all x1, starting transfers between devices, per_device(): lax.all_to_all(targets, 'node', split_axis=0, concat_axis=0, tiled=True)  13.7 us
  transfers between devices with their start and end apart: 5, of which 4 were waited for; matrix products, arithmetic and copies ran while one was open for 42% of the time, Pallas kernels for 0%

commit v1 on v0

v1 whole, which is shorter than its diff:
```python
import functools

import jax
import jax.numpy as jnp
from jax import lax
from jax.experimental import pallas as pl
from jax.experimental.pallas import tpu as pltpu
from jax.sharding import PartitionSpec as P

FAN2 = 10
NX, NZ = 4, 8
LANES = 128
CHUNK = 8
MESH = pl.DeviceIdType.MESH
F32, BF16 = jnp.float32, jnp.bfloat16


def tiles_kernel(src, dst, rows, x_ref, cols_ref, out_ref, deg_ref, xs, *accs):
    per_step = out_ref.shape[0]
    step = pl.program_id(0)
    feat = lax.axis_index("feat")
    slots = cols_ref.shape[0] // per_step
    depth = cols_ref.shape[1]

    @pl.when(step == 0)
    def _():
        for b in range(xs.shape[0]):
            xs[b] = x_ref[:, b * LANES : (b + 1) * LANES].astype(F32)

    lane = lax.broadcasted_iota(jnp.int32, (8, LANES), 1)

    def target(j, _):
        for acc in accs:
            acc[...] = jnp.zeros_like(acc)
        deg = jnp.zeros((8, LANES), F32)
        for c in range(slots // CHUNK):
            base = (step * per_step + j) * slots + c * CHUNK
            valid = [rows[base + i] for i in range(CHUNK)]

            def work(deg):
                sums = []
                for i in range(CHUNK):
                    block = xs[src[base + i]]
                    t = j * slots + c * CHUNK + i
                    total = None
                    for k in range(depth):
                        index = jnp.broadcast_to(cols_ref[t, pl.ds(k, 1), :], (8, LANES))
                        got = jnp.take_along_axis(block, index, axis=1, mode="promise_in_bounds")
                        total = got if total is None else total + got
                    sums.append(jnp.where(lane < valid[i], total, 0.0))
                for i in range(CHUNK):
                    acc, d = accs[i % len(accs)], dst[base + i]
                    acc[d] += sums[i]
                    deg += jnp.where(lane < jnp.where(d == feat, valid[i], 0), 1.0, 0.0)
                return deg

            deg = lax.cond(functools.reduce(lambda a, b: a + b, valid) > 0, work, lambda d: d, deg)
        total = accs[0][...]
        for acc in accs[1:]:
            total += acc[...]
        out_ref[j] = total.reshape(out_ref.shape[1:]).astype(out_ref.dtype)
        deg_ref[0, pl.ds((step * per_step + j) % NZ, 1), :] = deg[0:1]
        return 0

    lax.fori_loop(0, per_step, target, 0)


def tile_sums(src, dst, rows, x, cols, near_blocks):
    nodes = NX * NZ
    smem = pl.BlockSpec(memory_space=pltpu.SMEM)
    return pl.pallas_call(
        tiles_kernel,
        grid=(NX,),
        out_shape=(
            jax.ShapeDtypeStruct((nodes, near_blocks * 8, LANES), BF16),
            jax.ShapeDtypeStruct((NX, NZ, LANES), F32),
        ),
        in_specs=[
            smem,
            smem,
            smem,
            pl.BlockSpec(x.shape, lambda e: (0, 0)),
            pl.BlockSpec((cols.shape[0] // NX, *cols.shape[1:]), lambda e: (e, 0, 0)),
        ],
        out_specs=(
            pl.BlockSpec((NZ, near_blocks * 8, LANES), lambda e: (e, 0, 0)),
            pl.BlockSpec((1, NZ, LANES), lambda e: (e, 0, 0)),
        ),
        scratch_shapes=[pltpu.VMEM((x.shape[1] // LANES, 8, LANES), F32)]
        + [pltpu.VMEM((near_blocks, 8, LANES), F32)] * 2,
    )(src, dst, rows, x, cols)


def exchange_kernel(
    parts, degp, xnear, weights, nbrs, out,
    wall, a1, b1, a2, b2, ac, ao, bo, bc, dgot, zs, zr, degs, s2, r2, s3, hs, r3, rh, s4, r4,
    wsem, xsend, xrecv, dsend, drecv, zsend, zrecv, fsem,
):
    node, f = lax.axis_index("node"), lax.axis_index("feat")
    x, z = node // NZ, node % NZ
    nf = wall.shape[0]
    xp, xm, xo = (x + 1) % NX, (x + NX - 1) % NX, (x + 2) % NX
    half = a1.shape[1]
    body = 2 * half

    def at(xx=x, zz=z, ff=f):
        return {"node": xx * NZ + zz, "feat": ff}

    def send(source, target, send_sem, recv_sem, device):
        copy = pltpu.make_async_remote_copy(
            src_ref=source, dst_ref=target, send_sem=send_sem, recv_sem=recv_sem,
            device_id=device, device_id_type=MESH,
        )
        copy.start()

    def landed(ref, sem):
        pltpu.make_async_copy(ref, ref, sem).wait()

    def order(i):
        return (4 + (1 - 2 * (i % 2)) * ((i + 1) // 2)) % NZ

    def loop(n, fn):
        lax.fori_loop(0, n, lambda i, c: (fn(i), c)[1], 0)

    barrier = pltpu.get_barrier_semaphore()

    def greet(device):
        pl.semaphore_signal(barrier, inc=1, device_id=device, device_id_type=MESH)

    loop(NX - 1, lambda i: greet(at(xx=(x + 1 + i) % NX)))
    loop(NZ - 1, lambda i: greet(at(zz=(z + 1 + i) % NZ)))
    loop(nf - 1, lambda i: greet(at(ff=(f + 1 + i) % nf)))
    pl.semaphore_wait(barrier, NX - 1 + NZ - 1 + nf - 1)

    def first(i):
        zi = (z + order(i)) % NZ
        send(parts.at[xo, zi, pl.ds(0, half)], a1.at[zi], xsend.at[0, zi], xrecv.at[0, zi], at(xx=xp))
        send(parts.at[xo, zi, pl.ds(half, half)], b1.at[zi], xsend.at[1, zi], xrecv.at[1, zi], at(xx=xm))

    loop(NZ, first)

    def degrees(i):
        xx = (x + 1 + i) % NX
        send(degp.at[xx], dgot.at[i], dsend.at[i], drecv.at[i], at(xx=xx))

    loop(NX - 1, degrees)

    def direct(i):
        zi = (z + order(i)) % NZ
        send(parts.at[xp, zi, pl.ds(half, half)], bo.at[zi], xsend.at[2, zi], xrecv.at[2, zi], at(xx=xp))
        send(parts.at[xm, zi, pl.ds(0, half)], ao.at[zi], xsend.at[3, zi], xrecv.at[3, zi], at(xx=xm))

    loop(NZ, direct)

    wall[f] = weights[...]
    loop(
        nf - 1,
        lambda i: send(weights, wall.at[f], wsem.at[0], wsem.at[1], at(ff=(f + 1 + i) % nf)),
    )

    def relay(i):
        zi = (z + order(i)) % NZ
        landed(a1.at[zi], xrecv.at[0, zi])
        a2[zi] = (a1[zi].astype(F32) + parts[xp, zi, pl.ds(0, half), :].astype(F32)).astype(BF16)
        send(a2.at[zi], ac.at[zi], xsend.at[4, zi], xrecv.at[4, zi], at(xx=xp))
        landed(b1.at[zi], xrecv.at[1, zi])
        b2[zi] = (b1[zi].astype(F32) + parts[xm, zi, pl.ds(half, half), :].astype(F32)).astype(BF16)
        send(b2.at[zi], bc.at[zi], xsend.at[5, zi], xrecv.at[5, zi], at(xx=xm))

    loop(NZ, relay)

    near = nbrs[...]
    columns = lax.broadcasted_iota(jnp.int32, (near.shape[0], LANES), 1) + f * LANES
    counts = jnp.zeros((near.shape[0], LANES), F32)
    for n in range(FAN2):
        counts += jnp.where(near[:, n : n + 1] == columns, 1.0, 0.0)
    counts = counts.astype(BF16)
    for b in range(nf):
        s2[b, 0:8] = xnear[:, b * LANES : (b + 1) * LANES].astype(F32)

    for i in range(NX - 1):
        landed(dgot.at[i], drecv.at[i])
    deg_x = degp[x] + dgot[0] + dgot[1] + dgot[2]
    deg_tile = jnp.concatenate([deg_x, jnp.zeros_like(deg_x)], axis=0).astype(BF16)

    def onward(i):
        dz = order(i)
        zi = (z + dz) % NZ
        for kind, ref in ((2, bo), (3, ao), (4, ac), (5, bc)):
            landed(ref.at[zi], xrecv.at[kind, zi])
        zs[zi, 0:half] = (
            parts[x, zi, pl.ds(0, half), :].astype(F32) + ao[zi].astype(F32) + ac[zi].astype(F32)
        ).astype(BF16)
        zs[zi, half:body] = (
            parts[x, zi, pl.ds(half, half), :].astype(F32) + bo[zi].astype(F32) + bc[zi].astype(F32)
        ).astype(BF16)
        zs[zi, body : body + 16] = deg_tile

        @pl.when(dz != 0)
        def _():
            send(zs.at[zi], zr.at[dz - 1], zsend.at[dz - 1], zrecv.at[dz - 1], at(zz=zi))

    loop(NZ, onward)

    own = zs[z]
    agg = own[0:body].astype(F32)
    deg = own[body : body + 16].astype(F32)
    for i in (3, 2, 4, 1, 5, 0, 6):
        landed(zr.at[i], zrecv.at[i])
        got = zr[i]
        agg += got[0:body].astype(F32)
        deg += got[body : body + 16].astype(F32)
    degs[...] = deg
    for b in range(nf):
        s2[b, 8:16] = agg[b * 8 : b * 8 + 8]

    r2[f] = s2[f]

    def spread(i):
        p = (f + 1 + i) % nf
        send(s2.at[p], r2.at[f], fsem.at[0], fsem.at[1], at(ff=p))

    loop(nf - 1, spread)
    scale = 1.0 / jnp.maximum(4.0 * degs[pl.ds(z, 1), :], 1.0)
    landed(r2.at[pl.ds(0, nf - 1)], fsem.at[1])
    both = r2[...].reshape(nf * 16, LANES)
    is_sum = lax.broadcasted_iota(jnp.int32, both.shape, 0) % 16 >= 8
    both = jnp.where(is_sum, both * scale, both).astype(BF16)
    landed(wall.at[pl.ds(0, nf - 1)], wsem.at[1])
    w1 = wall[:, 0:16, :].reshape(nf * 16, wall.shape[2])
    pre = lax.dot_general(both, w1, (((0,), (0,)), ((), ())), preferred_element_type=F32)
    hidden = jnp.maximum(pre, 0.0).astype(BF16)
    s3[...] = jnp.dot(counts, hidden, preferred_element_type=F32)

    @pl.when(f == 0)
    def _():
        hs[...] = hidden.astype(F32)

    def seeds_out(i):
        p = (f + 1 + i) % nf
        send(s3.at[pl.ds(p * 8, 8)], r3.at[f], fsem.at[2], fsem.at[3], at(ff=p))

        @pl.when(f == 0)
        def _():
            send(hs.at[pl.ds(p * 8, 8)], rh, fsem.at[4], fsem.at[5], at(ff=p))

    loop(nf - 1, seeds_out)
    r3[f] = s3[pl.ds(f * 8, 8), :]
    landed(r3.at[pl.ds(0, nf - 1)], fsem.at[3])
    mean = jnp.zeros(r3.shape[1:], F32)
    for p in range(nf):
        mean += r3[p]
    mean = (mean / FAN2).astype(BF16)

    @pl.when(f == 0)
    def _():
        rh[...] = hs[0:8, :]

    @pl.when(f != 0)
    def _():
        landed(rh, fsem.at[5])

    w2s = wall[:, 16:32, :].reshape(nf * 16, wall.shape[2])
    w2n = wall[:, 32:48, :].reshape(nf * 16, wall.shape[2])
    logits = jnp.dot(rh[...].astype(BF16), w2s, preferred_element_type=F32) + jnp.dot(
        mean, w2n, preferred_element_type=F32
    )
    s4[...] = logits
    r4[f] = logits
    loop(nf - 1, lambda i: send(s4, r4.at[f], fsem.at[6], fsem.at[7], at(ff=(f + 1 + i) % nf)))

    def sent(i):
        for kind, ref in ((0, a1), (1, b1), (2, bo), (3, ao), (4, ac), (5, bc)):
            landed(ref.at[i], xsend.at[kind, i])

    loop(NZ, sent)
    for i in range(NX - 1):
        landed(dgot.at[i], dsend.at[i])
    for i in range(NZ - 1):
        landed(zr.at[i], zsend.at[i])
    landed(wall.at[pl.ds(0, nf - 1)], wsem.at[0])
    landed(r2.at[pl.ds(0, nf - 1)], fsem.at[0])
    landed(r3.at[pl.ds(0, nf - 1)], fsem.at[2])

    @pl.when(f == 0)
    def _():
        landed(hs.at[pl.ds(0, 8 * (nf - 1))], fsem.at[4])

    landed(r4.at[pl.ds(0, nf - 1)], fsem.at[7])
    out[...] = r4[...]
    landed(r4.at[pl.ds(0, nf - 1)], fsem.at[6])


def exchange(parts, degp, xnear, weights, nbrs, feats, seeds):
    hid = weights.shape[1]
    rows = parts.shape[2]
    half = rows // 2
    vm = pl.BlockSpec(memory_space=pltpu.VMEM)
    quarter = pltpu.VMEM((NZ, half, LANES), BF16)
    dma = pltpu.SemaphoreType.DMA
    return pl.pallas_call(
        exchange_kernel,
        out_shape=jax.ShapeDtypeStruct((feats, 8, hid), F32),
        in_specs=[vm] * 5,
        out_specs=vm,
        scratch_shapes=[
            pltpu.VMEM((feats, *weights.shape), BF16),
            *[quarter] * 8,
            pltpu.VMEM((NX - 1, NZ, LANES), F32),
            pltpu.VMEM((NZ, rows + 16, LANES), BF16),
            pltpu.VMEM((NZ - 1, rows + 16, LANES), BF16),
            pltpu.VMEM((16, LANES), F32),
            pltpu.VMEM((feats, 16, LANES), F32),
            pltpu.VMEM((feats, 16, LANES), F32),
            pltpu.VMEM((seeds, hid), F32),
            pltpu.VMEM((LANES, hid), F32),
            pltpu.VMEM((feats, 8, hid), F32),
            pltpu.VMEM((8, hid), F32),
            pltpu.VMEM((8, hid), F32),
            pltpu.VMEM((feats, 8, hid), F32),
            dma((2,)),
            dma((6, NZ)),
            dma((6, NZ)),
            dma((NX - 1,)),
            dma((NX - 1,)),
            dma((NZ - 1,)),
            dma((NZ - 1,)),
            dma((8,)),
        ],
        compiler_params=pltpu.CompilerParams(
            collective_id=0, has_side_effects=True, vmem_limit_bytes=32 * 1024 * 1024
        ),
    )(parts, degp, xnear, weights, nbrs)


def loss_kernel(table, labels, logits, loss):
    full = jnp.transpose(table[...])
    rows = full[0 : logits.shape[0]]
    logits[...] = rows
    classes = lax.broadcasted_iota(jnp.int32, rows.shape, 0)
    picked = jnp.sum(jnp.where(classes == labels[...], rows, 0.0), axis=0, keepdims=True)
    loss[...] = jnp.log(jnp.sum(jnp.exp(rows), axis=0, keepdims=True)) - picked


def per_device(
    x_far,
    x_near,
    tile_src,
    tile_dst,
    tile_rows,
    tile_cols,
    seed_nbrs,
    labels,
    self_one,
    neigh_one,
    self_two,
    neigh_two,
):
    feats = lax.axis_size("feat")
    hid = self_one.shape[0]
    classes = self_two.shape[0]
    seeds = labels.shape[0]
    near_blocks = x_near.shape[1] // LANES
    pad = ((0, 0), (0, hid - classes))
    weights = jnp.concatenate(
        [self_one.T, neigh_one.T, jnp.pad(self_two.T, pad), jnp.pad(neigh_two.T, pad)], axis=0
    )
    parts, degp = tile_sums(tile_src, tile_dst, tile_rows, x_far, tile_cols, near_blocks)
    parts = parts.reshape(NX, NZ, near_blocks * 8, LANES)
    table = exchange(parts, degp, x_near, weights, seed_nbrs, feats, seeds)
    logits, loss = pl.pallas_call(
        loss_kernel,
        out_shape=(
            jax.ShapeDtypeStruct((classes, seeds), F32),
            jax.ShapeDtypeStruct((1, seeds), F32),
        ),
    )(table.reshape(seeds, hid), labels.reshape(1, seeds))
    return logits, loss.reshape(seeds)


def solution(mesh):
    placed = (
        P("feat", "node"),
        P("feat", "node"),
        P("node"),
        P("node"),
        P("node"),
        P("node", None, None),
        P("node", None),
        P("node"),
        P(None, "feat"),
        P(None, "feat"),
        P(None, "feat"),
        P(None, "feat"),
    )
    return jax.shard_map(
        per_device,
        mesh=mesh,
        in_specs=placed,
        out_specs=(P(None, "node"), P("node")),
        check_vma=False,
    )
```

time: 556 us -> 73.5 us (0.13)
  waiting for transfers between devices: 265 us -> 0 us
  other arithmetic: 104 us -> 0.75 us
  local copies, waits for them, and re-layouts: 86.5 us -> 3.38 us
  Pallas kernels: 0 us -> 68.4 us
  matrix products: 55.5 us -> 0 us
  starting transfers between devices: 27.1 us -> 0 us
  between operations: 14.2 us -> 0.66 us
    psum x1 -> x0, waiting for transfers between devices: 110 us -> none  [per_device(): logits = lax.psum(part_logits, 'feat')]
    reduce_sum x34 -> x0, other arithmetic: 97.7 us -> none  [the longest x32 95.5 us: tile_counts(): hits = jnp.sum((cols[..., None] == lanes).astype(jnp.bfloat16), axis=1)]
    all_to_all x3 -> x0, waiting for transfers between devices: 95.1 us -> none  [the longest x1 89.5 us: per_device(): lax.all_to_all(partial_value, 'node', split_axis=0, concat_axis=0, tiled=...]
    pallas_call x0 -> x3, Pallas kernels: none -> 68.4 us  [the longest x1 51.2 us: exchange(): pl.pallas_call(exchange_kernel, out_shape=jax.ShapeDtypeStruct((feats, 8,...]
    reduce_scatter x1 -> x0, waiting for transfers between devices: 59.2 us -> none  [per_device(): z_share = lax.psum_scatter(z_part, 'feat', scatter_dimension=0, tiled=True)]
    dot_general x38 -> x0, matrix products: 55.5 us -> none  [the longest x32 50.1 us: group(): jnp.einsum('fgc,grc->gfr', chosen, counts, preferred_element_type=jnp.flo...]
    gather x32 -> x0, local copies, waits for them, and re-layouts: 49.4 us -> none  [group(): chosen = jnp.take(blocks, src_g, axis=1)]
    eq x33 -> x0, local copies, waits for them, and re-layouts: 27.3 us -> none  [the longest x32 27.2 us: tile_counts(): hits = jnp.sum((cols[..., None] == lanes).astype(jnp.bfloat16), axis=1)]
  transfers between devices with their start and end apart: 5 -> 0, of which waited for: 4 -> 0; matrix products, arithmetic and copies ran while one was open for 42% -> 0% of each run, Pallas kernels for 0% -> 0%
where the time goes in v1:
time: 73.5 us; the launch traced here: 73.2 us
  Pallas kernels  68.4 us (93%)
  local copies, waits for them, and re-layouts  3.38 us (5%)
  other arithmetic  0.75 us (1%)
    pallas_call x1, Pallas kernels, exchange(): pl.pallas_call(exchange_kernel, out_shape=jax.ShapeDtypeStruct((feats, 8,...  51.2 us
    pallas_call x1, Pallas kernels, tile_sums(): pl.pallas_call(tiles_kernel, grid=(NX,), out_shape=(jax.ShapeDtypeStruct(...  15.5 us
    unnamed x9, local copies, waits for them, and re-layouts  3.38 us
    pallas_call x1, Pallas kernels, per_device(): pl.pallas_call(loss_kernel, out_shape=(jax.ShapeDtypeStruct((classes, see...  1.65 us

profile of v1, /device:TPU:1, one launch (start us, length us, event | category | flops | bytes accessed | tf_op | source)
XLA Modules:
  0.0 73.2 jit_solution(5663648023109695126)
XLA Ops:
  0.6 0.0 copy-start.2
  0.6 0.7 %fusion.4.weights = bf16[48,256]{1,0:T(8,128)(2,1)S(1)} fusion(bf16[16,172]{1,0:T(8,128)(2,1)} %bitcast.10, bf16[16,172]{1,0:T(8,128)(2,1)} %bitcast.11, bf16[8,256]{1,0:T(8,128)(2,1)} %bitcast.12, bf16[8,256]{1,0:T(8,128)(2,1)} %bitcast.13), kind=kLoop, calls=%fused_computation.7 | loop fusion | flops 172032 | bytes 43776 | tf_op jit(solution)/shard_map/concatenate | solution.py:365
  1.4 0.8 %copy.14.nbrs = s32[128,10]{1,0:T(8,128)S(1)} copy(s32[128,10]{0,1:T(8,128)} %param.18) | data formatting | bytes 10240 | tf_op args[6]
  2.2 15.5 %shard_map.131 = (bf16[32,128,128]{2,1,0:T(8,128)(2,1)}, f32[4,8,128]{2,1,0:T(8,128)}) custom-call(s32[1024]{0:T(1024)} %src.1, s32[1024]{0:T(1024)} %dst.1, s32[1024]{0:T(1024)} %rows.1, bf16[8,16384]{1,0:T(8,128)(2,1)} %x_ref.1, s32[1024,4,128]{2,1,0:T(4,128)} %cols_ref.1), custom_call_target="tpu_custom_call" | custom-call | tf_op jit(solution)/shard_map/pallas_call | solution.py:71
  17.7 0.0 copy-done.2
  17.7 0.0 copy-start
  17.7 1.2 %copy-done = bf16[32,128,128]{2,1,0:T(8,128)(2,1)S(1)} copy-done((bf16[32,128,128]{2,1,0:T(8,128)(2,1)S(1)}, bf16[32,128,128]{2,1,0:T(8,128)(2,1)}, u32[]{:S(2)}) %copy-start) | copy-done | bytes 1048600
  18.9 0.0 copy-start.3
  18.9 0.7 copy-done.3
  19.7 51.2 %shard_map.132 = f32[16,8,256]{2,1,0:T(8,128)S(1)} custom-call(bf16[4,8,128,128]{3,2,1,0:T(8,128)(2,1)S(1)} %bitcast.8, f32[4,8,128]{2,1,0:T(8,128)S(1)} %copy-done.3, bf16[8,2048]{1,0:T(8,128)(2,1)S(1)} %copy-done.2, bf16[48,256]{1,0:T(8,128)(2,1)S(1)} %fusion.4.weights, s32[128,10]{1,0:T(8,128)S(1)} %copy.14.nbrs), custom_call_target="tpu_custom_call" | custom-call | tf_op jit(solution)/shard_map/pallas_call | solution.py:301
  70.9 0.0 copy-start.1
  70.9 0.6 copy-done.1
  71.5 1.6 %shard_map.133 = (f32[172,128]{1,0:T(8,128)}, f32[1,128]{1,0:T(1,128)}) custom-call(f32[128,256]{1,0:T(8,128)} %bitcast.9, s32[1,128]{1,0:T(1,128)} %bitcast.14), custom_call_target="tpu_custom_call" | custom-call | tf_op jit(solution)/shard_map/pallas_call | solution.py:371
Async XLA Ops:
  0.6 17.1 %copy-start.2 = (bf16[8,2048]{1,0:T(8,128)(2,1)S(1)}, bf16[8,2048]{1,0:T(8,128)(2,1)}, u32[]{:S(2)}) copy-start(bf16[8,2048]{1,0:T(8,128)(2,1)} %xnear.1) | copy-start | bytes 98308
  17.7 1.2 %copy-start = (bf16[32,128,128]{2,1,0:T(8,128)(2,1)S(1)}, bf16[32,128,128]{2,1,0:T(8,128)(2,1)}, u32[]{:S(2)}) copy-start(bf16[32,128,128]{2,1,0:T(8,128)(2,1)} %get-tuple-element.6) | copy-start | bytes 3145732
  18.9 0.7 copy-start.3
  70.9 0.6 copy-start.1

commit v2 on v0

v2 whole, which is shorter than its diff:
```python
import functools

import jax
import jax.numpy as jnp
from jax import lax
from jax.experimental import pallas as pl
from jax.experimental.pallas import tpu as pltpu
from jax.sharding import PartitionSpec as P

FAN2 = 10
NX, NZ = 4, 8
LANES = 128
VMEM = 60 * 1024 * 1024
MESH = pl.DeviceIdType.MESH
F32, BF16 = jnp.float32, jnp.bfloat16


def plan_kernel(dst, rows, prev, last, degp):
    slots = 32
    d = dst[...]
    lane = lax.broadcasted_iota(jnp.int32, d.shape, 1)
    pos = lane % slots
    found = jnp.full(d.shape, slots, jnp.int32)
    for s in range(slots - 1, 0, -1):
        found = jnp.where((pos >= s) & (pltpu.roll(d, s, 1) == d), pos - s, found)
    prev[...] = found
    ends = jnp.full(d.shape, slots, jnp.int32)
    for b in range(16):
        v = jnp.where(d == b, pos, -1)
        for s in (1, 2, 4, 8, 16):
            v = jnp.maximum(v, jnp.where((pos & s) == 0, pltpu.roll(v, LANES - s, 1), pltpu.roll(v, s, 1)))
        ends = jnp.where((pos == b) & (v >= 0), v, ends)
    last[...] = ends
    mine = jnp.where(d == lax.axis_index("feat"), rows[...], 0).astype(F32)
    columns = jnp.transpose(jnp.concatenate([mine] * 16, axis=0))
    across = lax.broadcasted_iota(jnp.int32, (LANES, LANES), 1).astype(F32)
    for r in range(8):
        live = jnp.where(across < columns[:, r : r + 1], 1.0, 0.0)
        sums = jnp.sum(live.reshape(4, slots, LANES), axis=1)
        degp[r // 2, (r % 2) * 4 : (r % 2) * 4 + 4, :] = sums


def step_kernel(
    src, rows, prev, last, x_ref, cols, degp, xnear, self1, neigh1, self2, neigh2, nbrs, out,
    xs, cv, buf, parts, stage, weights, wall, a1, b1, a2, b2, ac, ao, bo, bc, dgot, degx, dz_got,
    zs, zr, near, sums, r2, s3, hs, r3, rh, s4, r4,
    csem, wsem, nsem, xsend, xrecv, dsem, esem, zsend, zrecv, fsem, gsend, grecv, psem,
):
    node, f = lax.axis_index("node"), lax.axis_index("feat")
    x, z = node // NZ, node % NZ
    y, core = f // 2, f % 2
    nf = wall.shape[0]
    xp, xm, xo = (x + 1) % NX, (x + NX - 1) % NX, (x + 2) % NX
    half = a1.shape[1]
    body = 2 * half
    slots, depth = cv.shape[2], cv.shape[3]

    def at(xx=x, zz=z, ff=f):
        return {"node": xx * NZ + zz, "feat": ff}

    def send(source, target, send_sem, recv_sem, device):
        copy = pltpu.make_async_remote_copy(
            src_ref=source, dst_ref=target, send_sem=send_sem, recv_sem=recv_sem,
            device_id=device, device_id_type=MESH,
        )
        copy.start()

    def landed(ref, sem):
        pltpu.make_async_copy(ref, ref, sem).wait()

    def order(i):
        return (4 + (1 - 2 * (i % 2)) * ((i + 1) // 2)) % NZ

    def loop(lo, hi, fn):
        lax.fori_loop(lo, hi, lambda i, c: (fn(i), c)[1], 0)

    barrier = pltpu.get_barrier_semaphore()

    def greet(device):
        pl.semaphore_signal(barrier, inc=1, device_id=device, device_id_type=MESH)

    loop(0, NX - 1, lambda i: greet(at(xx=(x + 1 + i) % NX)))
    loop(0, NZ - 1, lambda i: greet(at(zz=(z + 1 + i) % NZ)))
    loop(0, nf - 1, lambda i: greet(at(ff=(f + 1 + i) % nf)))

    def columns_in(i):
        zi = (z + order(i)) % NZ
        pltpu.make_async_copy(cols.at[:, zi], cv.at[:, zi], csem.at[i]).start()

    loop(0, NZ, columns_in)

    for b in range(xs.shape[0]):
        xs[b] = x_ref[:, b * LANES : (b + 1) * LANES].astype(F32)
    buf[...] = jnp.zeros_like(buf)
    for b in range(nf):
        near[b] = xnear[:, b * LANES : (b + 1) * LANES].astype(F32)
    stage[...] = jnp.zeros_like(stage)
    stage[0:8] = self1[...].astype(F32)
    stage[8:16] = neigh1[...].astype(F32)
    stage[16:32, 0 : self2.shape[1]] = self2[...].astype(F32)
    stage[32:48, 0 : neigh2.shape[1]] = neigh2[...].astype(F32)
    weights[...] = stage[...].astype(BF16)
    lane = lax.broadcasted_iota(jnp.int32, (8, LANES), 1)

    def tile_sums(n):
        i, q = n // NX, n % NX
        zi = (z + order(i)) % NZ
        xx = (x + 2 + NX - q) % NX
        base = (xx * NZ + zi) * slots
        for s in range(slots):
            block = xs[src[base + s]]
            got = []
            for k in range(depth):
                index = jnp.broadcast_to(cv[xx, zi, s, pl.ds(k, 1), :], (8, LANES))
                got.append(jnp.take_along_axis(block, index, axis=1, mode="promise_in_bounds"))
            total = functools.reduce(lambda a, b: a + b, got)
            buf[s] = jnp.where(lane < rows[base + s], total, 0.0) + buf[prev[base + s]]
        for b in range(0, nf, 2):
            pair = [buf[last[base + b]], buf[last[base + b + 1]]]
            parts[xx, zi, b * 8 : b * 8 + 16] = jnp.concatenate(pair, axis=0).astype(BF16)

    def first(i):
        zi = (z + order(i)) % NZ
        send(parts.at[xo, zi, pl.ds(0, half)], a1.at[zi], xsend.at[0, zi], xrecv.at[0, zi], at(xx=xp))
        send(parts.at[xo, zi, pl.ds(half, half)], b1.at[zi], xsend.at[1, zi], xrecv.at[1, zi], at(xx=xm))

    def direct_up(i):
        zi = (z + order(i)) % NZ
        send(parts.at[xp, zi, pl.ds(half, half)], bo.at[zi], xsend.at[2, zi], xrecv.at[2, zi], at(xx=xp))

    def direct_down(i):
        zi = (z + order(i)) % NZ
        send(parts.at[xm, zi, pl.ds(0, half)], ao.at[zi], xsend.at[3, zi], xrecv.at[3, zi], at(xx=xm))

    def relay(i):
        zi = (z + order(i)) % NZ
        landed(a1.at[zi], xrecv.at[0, zi])
        a2[zi] = (a1[zi].astype(F32) + parts[xp, zi, pl.ds(0, half), :].astype(F32)).astype(BF16)
        send(a2.at[zi], ac.at[zi], xsend.at[4, zi], xrecv.at[4, zi], at(xx=xp))
        landed(b1.at[zi], xrecv.at[1, zi])
        b2[zi] = (b1[zi].astype(F32) + parts[xm, zi, pl.ds(half, half), :].astype(F32)).astype(BF16)
        send(b2.at[zi], bc.at[zi], xsend.at[5, zi], xrecv.at[5, zi], at(xx=xm))

    def summed(i):
        zi = (z + order(i)) % NZ
        for kind, ref in ((2, bo), (3, ao), (4, ac), (5, bc)):
            landed(ref.at[zi], xrecv.at[kind, zi])
        upper = parts[x, zi, pl.ds(0, half), :].astype(F32) + ao[zi].astype(F32) + ac[zi].astype(F32)
        lower = parts[x, zi, pl.ds(half, half), :].astype(F32) + bo[zi].astype(F32) + bc[zi].astype(F32)
        return upper, lower

    def onward(i):
        dz = order(i)
        zi = (z + dz) % NZ
        upper, lower = summed(i)
        zs[dz - 1, 0:half] = upper.astype(BF16)
        zs[dz - 1, half:body] = lower.astype(BF16)
        send(zs.at[dz - 1], zr.at[dz - 1], zsend.at[dz - 1], zrecv.at[dz - 1], at(zz=zi))

    loop(0, NX, lambda n: (pl.when(n == 0)(lambda: landed(cv.at[:, 0], csem.at[0])), tile_sums(n)))

    pl.semaphore_wait(barrier, NX - 1 + NZ - 1 + nf - 1)
    first(0)
    for i in range(NX - 1):
        send(degp.at[(x + 1 + i) % NX], dgot.at[i], dsem.at[0, i], dsem.at[1, i], at(xx=(x + 1 + i) % NX))
    direct_up(0)
    direct_down(0)

    wall[f] = weights[...]
    r2[f, 0:8] = near[f]

    def early(i):
        p = (f + 1 + i) % nf
        send(near.at[p], r2.at[f, pl.ds(0, 8)], nsem.at[0, 0], nsem.at[1, f], at(ff=p))
        send(weights, wall.at[f], wsem.at[0], wsem.at[1], at(ff=p))

    loop(0, nf - 1, early)

    def step(n):
        i, q = n // NX, n % NX

        @pl.when(q == 0)
        def _():
            landed(cv.at[:, 0], csem.at[i])

        tile_sums(n)

        @pl.when(q == 0)
        def _():
            first(i)

        @pl.when(q == 1)
        def _():
            direct_up(i)
            relay(i - 1)

        @pl.when((q == 2) & (i >= 2))
        def _():
            onward(i - 2)

        @pl.when(q == 3)
        def _():
            direct_down(i)

        @pl.when(n == NX + 3)
        def _():
            for j in range(NX - 1):
                landed(dgot.at[j], dsem.at[1, j])
            degx[...] = degp[x] + dgot[0] + dgot[1] + dgot[2]
            for dz in range(1, NZ):
                send(degx, dz_got.at[dz - 1], esem.at[0, dz - 1], esem.at[1, dz - 1], at(zz=(z + dz) % NZ))

    loop(NX, NX * NZ, step)
    relay(NZ - 1)
    onward(NZ - 2)

    own_nodes = lax.broadcasted_iota(jnp.int32, (LANES, nbrs.shape[1]), 0) + f * LANES
    counts = jnp.zeros(own_nodes.shape, F32)
    for n in range(FAN2):
        counts += jnp.where(nbrs[n : n + 1, :] == own_nodes, 1.0, 0.0)
    counts = counts.astype(BF16)
    deg = degx[pl.ds(z, 1), :]
    for i in range(NZ - 1):
        landed(dz_got.at[i], esem.at[1, i])
        deg += dz_got[i, pl.ds(z, 1), :]
    deg = jnp.maximum(4.0 * deg, 1.0)

    upper, lower = summed(NZ - 1)
    for i in (3, 2, 4, 1, 5, 0, 6):
        landed(zr.at[i], zrecv.at[i])
        upper += zr[i, 0:half].astype(F32)
        lower += zr[i, half:body].astype(F32)
    for b in range(nf // 2):
        sums[b] = upper[b * 8 : b * 8 + 8]
        sums[b + nf // 2] = lower[b * 8 : b * 8 + 8]

    def spread(i):
        p = (f + 1 + i) % nf
        send(sums.at[p], r2.at[f, pl.ds(8, 8)], fsem.at[0], fsem.at[1], at(ff=p))

    loop(0, nf - 1, spread)
    r2[f, 8:16] = sums[f]
    landed(wall.at[pl.ds(0, nf - 1)], wsem.at[1])

    def near_in(i):
        p = (f + 1 + i) % nf
        landed(near.at[p], nsem.at[1, p])

    loop(0, nf - 1, near_in)
    landed(sums.at[pl.ds(0, nf - 1)], fsem.at[1])
    both = r2[...].reshape(nf * 16, LANES)
    is_sum = lax.broadcasted_iota(jnp.int32, both.shape, 0) % 16 >= 8
    both = jnp.where(is_sum, both / deg, both).astype(BF16)
    w1 = wall[:, 0:16, :].reshape(nf * 16, wall.shape[2])
    pre = lax.dot_general(both, w1, (((0,), (0,)), ((), ())), preferred_element_type=F32)
    hidden = jnp.maximum(pre, 0.0).astype(BF16)
    seed_sums = lax.dot_general(counts, hidden, (((0,), (0,)), ((), ())), preferred_element_type=F32)
    for p in range(nf):
        piece = seed_sums[p * 8 : p * 8 + 8]
        s3[p] = jnp.concatenate([piece[:, 0:LANES], piece[:, LANES:]], axis=0).astype(BF16)

    @pl.when(f == 0)
    def _():
        wide = hidden.astype(F32)
        for p in range(nf):
            piece = wide[p * 8 : p * 8 + 8]
            hs[p] = jnp.concatenate([piece[:, 0:LANES], piece[:, LANES:]], axis=0).astype(BF16)

    def seeds_out(i):
        p = (f + 1 + i) % nf
        send(s3.at[p], r3.at[f], fsem.at[2], fsem.at[3], at(ff=p))

        @pl.when(f == 0)
        def _():
            send(hs.at[p], rh, fsem.at[4], fsem.at[5], at(ff=p))

    loop(0, nf - 1, seeds_out)
    r3[f] = s3[f]

    @pl.when(f == 0)
    def _():
        rh[...] = hs[0]

    @pl.when(f != 0)
    def _():
        landed(rh, fsem.at[5])

    w2s = wall[:, 16:32, :].reshape(nf * 16, wall.shape[2])
    w2n = wall[:, 32:48, :].reshape(nf * 16, wall.shape[2])

    def rejoin(v):
        return jnp.concatenate([v[0:8], v[8:16]], axis=1).astype(BF16)

    logits = jnp.dot(rejoin(rh[...].astype(F32)), w2s, preferred_element_type=F32)
    landed(s3.at[pl.ds(0, nf - 1)], fsem.at[3])
    mean = jnp.zeros(r3.shape[1:], F32)
    for p in range(nf):
        mean += r3[p].astype(F32)
    logits += jnp.dot(rejoin(mean / FAN2), w2n, preferred_element_type=F32)

    s4[...] = logits
    other = at(ff=f + 1 - 2 * core)

    def along(i):
        yy = (y + 1 + i) % (nf // 2)
        send(s4, r4.at[core, y], gsend.at[i], grecv.at[y], at(ff=yy * 2 + core))

    loop(0, nf // 2 - 1, along)
    send(s4, r4.at[core, y], gsend.at[nf // 2 - 1], psem.at[1, y], other)
    r4[core, y] = logits

    def across(i):
        yy = (y + nf + (1 - 2 * (i % 2)) * (i // 2 + 1)) % (nf // 2)
        landed(s4, grecv.at[yy])
        send(r4.at[core, yy], r4.at[core, yy], psem.at[0, i], psem.at[1, yy], other)

    loop(0, nf // 2 - 1, across)

    def sent(i):
        for kind, ref in ((0, a1), (1, b1), (2, bo), (3, ao), (4, ac), (5, bc)):
            landed(ref.at[i], xsend.at[kind, i])

    loop(0, NZ, sent)
    for i in range(NX - 1):
        landed(dgot.at[i], dsem.at[0, i])
    for i in range(NZ - 1):
        landed(zr.at[i], zsend.at[i])
        landed(dz_got.at[i], esem.at[0, i])
    landed(wall.at[pl.ds(0, nf - 1)], wsem.at[0])
    landed(near.at[pl.ds(0, nf - 1)], nsem.at[0, 0])
    landed(sums.at[pl.ds(0, nf - 1)], fsem.at[0])
    landed(s3.at[pl.ds(0, nf - 1)], fsem.at[2])

    @pl.when(f == 0)
    def _():
        landed(hs.at[pl.ds(0, nf - 1)], fsem.at[4])

    for i in range(nf // 2):
        landed(s4, gsend.at[i])
        landed(s4, psem.at[1, i])
    for i in range(nf // 2 - 1):
        landed(s4, psem.at[0, i])
    for i in range(nf):
        out[i] = r4[i % 2, i // 2]


def tile_plan(dst, rows):
    shape = (8, LANES)
    ints = jax.ShapeDtypeStruct(shape, jnp.int32)
    return pl.pallas_call(
        plan_kernel,
        out_shape=(ints, ints, jax.ShapeDtypeStruct((NX, NZ, LANES), F32)),
        compiler_params=pltpu.CompilerParams(vmem_limit_bytes=VMEM),
    )(dst.reshape(shape), rows.reshape(shape))


def seed_logits(src, rows, x, cols, degp, prev, last, xnear, w, nbrs, feats):
    self1, neigh1, self2, neigh2 = w
    hid = self1.shape[1]
    seeds = nbrs.shape[1]
    slots, depth = cols.shape[0] // (NX * NZ), cols.shape[1]
    body = feats * 8
    half = body // 2
    vm = pl.BlockSpec(memory_space=pltpu.VMEM)
    sm = pl.BlockSpec(memory_space=pltpu.SMEM)
    quarter = pltpu.VMEM((NZ, half, LANES), BF16)
    dma = pltpu.SemaphoreType.DMA
    return pl.pallas_call(
        step_kernel,
        out_shape=jax.ShapeDtypeStruct((feats, seeds // feats, hid), F32),
        in_specs=[sm] * 4 + [vm, pl.BlockSpec(memory_space=pl.ANY)] + [vm] * 7,
        out_specs=vm,
        scratch_shapes=[
            pltpu.VMEM((x.shape[1] // LANES, 8, LANES), F32),
            pltpu.VMEM((NX, NZ, slots, depth, LANES), jnp.int32),
            pltpu.VMEM((slots + 1, 8, LANES), F32),
            pltpu.VMEM((NX, NZ, body, LANES), BF16),
            pltpu.VMEM((48, hid), F32),
            pltpu.VMEM((48, hid), BF16),
            pltpu.VMEM((feats, 48, hid), BF16),
            *[quarter] * 8,
            pltpu.VMEM((NX - 1, NZ, LANES), F32),
            pltpu.VMEM((NZ, LANES), F32),
            pltpu.VMEM((NZ - 1, NZ, LANES), F32),
            pltpu.VMEM((NZ - 1, body, LANES), BF16),
            pltpu.VMEM((NZ - 1, body, LANES), BF16),
            pltpu.VMEM((feats, 8, LANES), F32),
            pltpu.VMEM((feats, 8, LANES), F32),
            pltpu.VMEM((feats, 16, LANES), F32),
            pltpu.VMEM((feats, 16, LANES), BF16),
            pltpu.VMEM((feats, 16, LANES), BF16),
            pltpu.VMEM((feats, 16, LANES), BF16),
            pltpu.VMEM((16, LANES), BF16),
            pltpu.VMEM((8, hid), F32),
            pltpu.VMEM((2, feats // 2, 8, hid), F32),
            dma((NZ,)),
            dma((2,)),
            dma((2, feats)),
            dma((6, NZ)),
            dma((6, NZ)),
            dma((2, NX - 1)),
            dma((2, NZ - 1)),
            dma((NZ - 1,)),
            dma((NZ - 1,)),
            dma((6,)),
            dma((feats // 2,)),
            dma((feats // 2,)),
            dma((2, feats // 2)),
        ],
        compiler_params=pltpu.CompilerParams(
            collective_id=0, has_side_effects=True, vmem_limit_bytes=VMEM
        ),
    )(
        src, rows, prev.reshape(-1), last.reshape(-1), x, cols.reshape(NX, NZ, slots, depth, LANES),
        degp, xnear, self1, neigh1, self2, neigh2, nbrs,
    )


def loss_kernel(table, labels, logits, loss):
    full = jnp.transpose(table[...])
    rows = full[0 : logits.shape[0]]
    logits[...] = rows
    classes = lax.broadcasted_iota(jnp.int32, rows.shape, 0)
    picked = jnp.sum(jnp.where(classes == labels[...], rows, 0.0), axis=0, keepdims=True)
    loss[...] = jnp.log(jnp.sum(jnp.exp(rows), axis=0, keepdims=True)) - picked


def per_device(
    x_far,
    x_near,
    tile_src,
    tile_dst,
    tile_rows,
    tile_cols,
    seed_nbrs,
    labels,
    self_one,
    neigh_one,
    self_two,
    neigh_two,
):
    feats = lax.axis_size("feat")
    classes, hid = self_two.shape[0], self_one.shape[0]
    seeds = labels.shape[0]
    prev, last, degp = tile_plan(tile_dst, tile_rows)
    weights = (self_one.T, neigh_one.T, self_two.T, neigh_two.T)
    table = seed_logits(
        tile_src, tile_rows, x_far, tile_cols, degp, prev, last, x_near, weights, seed_nbrs.T, feats
    )
    logits, loss = pl.pallas_call(
        loss_kernel,
        out_shape=(
            jax.ShapeDtypeStruct((classes, seeds), F32),
            jax.ShapeDtypeStruct((1, seeds), F32),
        ),
        compiler_params=pltpu.CompilerParams(vmem_limit_bytes=VMEM),
    )(table.reshape(seeds, hid), labels.reshape(1, seeds))
    return logits, loss.reshape(seeds)


def solution(mesh):
    placed = (
        P("feat", "node"),
        P("feat", "node"),
        P("node"),
        P("node"),
        P("node"),
        P("node", None, None),
        P("node", None),
        P("node"),
        P(None, "feat"),
        P(None, "feat"),
        P(None, "feat"),
        P(None, "feat"),
    )
    return jax.shard_map(
        per_device,
        mesh=mesh,
        in_specs=placed,
        out_specs=(P(None, "node"), P("node")),
        check_vma=False,
    )
```

time: 556 us -> 66.2 us (0.12)
  waiting for transfers between devices: 265 us -> 0 us
  other arithmetic: 104 us -> 0 us
  local copies, waits for them, and re-layouts: 86.5 us -> 0 us
  Pallas kernels: 0 us -> 65.4 us
  matrix products: 55.5 us -> 0 us
  starting transfers between devices: 27.1 us -> 0 us
  between operations: 14.2 us -> 0.64 us
    psum x1 -> x0, waiting for transfers between devices: 110 us -> none  [per_device(): logits = lax.psum(part_logits, 'feat')]
    reduce_sum x34 -> x0, other arithmetic: 97.7 us -> none  [the longest x32 95.5 us: tile_counts(): hits = jnp.sum((cols[..., None] == lanes).astype(jnp.bfloat16), axis=1)]
    all_to_all x3 -> x0, waiting for transfers between devices: 95.1 us -> none  [the longest x1 89.5 us: per_device(): lax.all_to_all(partial_value, 'node', split_axis=0, concat_axis=0, tiled=...]
    pallas_call x0 -> x3, Pallas kernels: none -> 65.4 us  [the longest x1 61.4 us: seed_logits(): pl.pallas_call(step_kernel, out_shape=jax.ShapeDtypeStruct((feats, seeds...]
    reduce_scatter x1 -> x0, waiting for transfers between devices: 59.2 us -> none  [per_device(): z_share = lax.psum_scatter(z_part, 'feat', scatter_dimension=0, tiled=True)]
    dot_general x38 -> x0, matrix products: 55.5 us -> none  [the longest x32 50.1 us: group(): jnp.einsum('fgc,grc->gfr', chosen, counts, preferred_element_type=jnp.flo...]
    gather x32 -> x0, local copies, waits for them, and re-layouts: 49.4 us -> none  [group(): chosen = jnp.take(blocks, src_g, axis=1)]
    eq x33 -> x0, local copies, waits for them, and re-layouts: 27.3 us -> none  [the longest x32 27.2 us: tile_counts(): hits = jnp.sum((cols[..., None] == lanes).astype(jnp.bfloat16), axis=1)]
  transfers between devices with their start and end apart: 5 -> 0, of which waited for: 4 -> 0; matrix products, arithmetic and copies ran while one was open for 42% -> 0% of each run, Pallas kernels for 0% -> 0%
where the time goes in v2:
time: 66.2 us; the launch traced here: 66 us
  Pallas kernels  65.4 us (99%)
    pallas_call x1, Pallas kernels, seed_logits(): pl.pallas_call(step_kernel, out_shape=jax.ShapeDtypeStruct((feats, seeds...  61.4 us
    pallas_call x1, Pallas kernels, tile_plan(): pl.pallas_call(plan_kernel, out_shape=(ints, ints, jax.ShapeDtypeStruct((...  2.35 us
    pallas_call x1, Pallas kernels, per_device(): pl.pallas_call(loss_kernel, out_shape=(jax.ShapeDtypeStruct((classes, see...  1.65 us

profile of v2, /device:TPU:1, one launch (start us, length us, event | category | flops | bytes accessed | tf_op | source)
XLA Modules:
  0.0 66.0 jit_solution(15477369994198465811)
XLA Ops:
  0.6 2.4 %shard_map.131 = (s32[8,128]{1,0:T(8,128)}, s32[8,128]{1,0:T(8,128)}, f32[4,8,128]{2,1,0:T(8,128)}) custom-call(s32[8,128]{1,0:T(8,128)} %bitcast.23, s32[8,128]{1,0:T(8,128)} %bitcast.15), custom_call_target="tpu_custom_call" | custom-call | tf_op jit(solution)/shard_map/pallas_call | solution.py:350
  3.0 61.4 %shard_map.132 = f32[16,8,256]{2,1,0:T(8,128)} custom-call(s32[1024]{0:T(1024)} %src.1, s32[1024]{0:T(1024)} %rows.1, s32[1024]{0:T(1024)} %bitcast.21, s32[1024]{0:T(1024)} %bitcast.22, bf16[8,16384]{1,0:T(8,128)(2,1)} %x_ref.1, s32[4,8,32,4,128]{4,3,2,1,0:T(4,128)} %bitcast.13, f32[4,8,128]{2,1,0:T(8,128)} %get-tuple-element.9.degp, ...), custom_call_target="tpu_custom_call" | custom-call | tf_op jit(solution)/shard_map/pallas_call | solution.py:368
  64.4 1.6 %shard_map.133 = (f32[172,128]{1,0:T(8,128)}, f32[1,128]{1,0:T(1,128)}) custom-call(f32[128,256]{1,0:T(8,128)} %bitcast.14, s32[1,128]{1,0:T(1,128)} %bitcast.24), custom_call_target="tpu_custom_call" | custom-call | tf_op jit(solution)/shard_map/pallas_call | solution.py:450

commit v3 on v2

--- a/solution.py
+++ b/solution.py
@@ -102,18 +102,34 @@
     weights[...] = stage[...].astype(BF16)
     lane = lax.broadcasted_iota(jnp.int32, (8, LANES), 1)
 
-    def tile_sums(n):
-        i, q = n // NX, n % NX
-        zi = (z + order(i)) % NZ
-        xx = (x + 2 + NX - q) % NX
+    rows_of = lax.broadcasted_iota(jnp.int32, (16, LANES), 0)
+    ids = [(rows_of + 16 * g).astype(jnp.int16) for g in range(LANES // 16)]
+    one, zero = jnp.ones((16, LANES), BF16), jnp.zeros((16, LANES), BF16)
+
+    def gathered(block, xx, zi, s):
+        got = []
+        for k in range(depth):
+            index = jnp.broadcast_to(cv[xx, zi, s, pl.ds(k, 1), :], (8, LANES))
+            got.append(jnp.take_along_axis(block, index, axis=1, mode="promise_in_bounds"))
+        return functools.reduce(lambda a, b: a + b, got)
+
+    def counted(block, xx, zi, s):
+        index = [
+            jnp.broadcast_to(cv[xx, zi, s, pl.ds(k, 1), :], (16, LANES)).astype(jnp.int16)
+            for k in range(depth)
+        ]
+        groups = []
+        for g in ids:
+            hits = [jnp.where(row == g, one, zero) for row in index]
+            groups.append(functools.reduce(lambda a, b: a + b, hits))
+        matrix = jnp.concatenate(groups, axis=0)
+        return jnp.dot(block.astype(BF16), matrix, preferred_element_type=F32)
+
+    def tile_sums(xx, zi):
         base = (xx * NZ + zi) * slots
         for s in range(slots):
             block = xs[src[base + s]]
-            got = []
-            for k in range(depth):
-                index = jnp.broadcast_to(cv[xx, zi, s, pl.ds(k, 1), :], (8, LANES))
-                got.append(jnp.take_along_axis(block, index, axis=1, mode="promise_in_bounds"))
-            total = functools.reduce(lambda a, b: a + b, got)
+            total = (counted if s % 2 else gathered)(block, xx, zi, s)
             buf[s] = jnp.where(lane < rows[base + s], total, 0.0) + buf[prev[base + s]]
         for b in range(0, nf, 2):
             pair = [buf[last[base + b]], buf[last[base + b + 1]]]
@@ -132,11 +148,14 @@
         zi = (z + order(i)) % NZ
         send(parts.at[xm, zi, pl.ds(0, half)], ao.at[zi], xsend.at[3, zi], xrecv.at[3, zi], at(xx=xm))
 
-    def relay(i):
+    def relay_up(i):
         zi = (z + order(i)) % NZ
         landed(a1.at[zi], xrecv.at[0, zi])
         a2[zi] = (a1[zi].astype(F32) + parts[xp, zi, pl.ds(0, half), :].astype(F32)).astype(BF16)
         send(a2.at[zi], ac.at[zi], xsend.at[4, zi], xrecv.at[4, zi], at(xx=xp))
+
+    def relay_down(i):
+        zi = (z + order(i)) % NZ
         landed(b1.at[zi], xrecv.at[1, zi])
         b2[zi] = (b1[zi].astype(F32) + parts[xm, zi, pl.ds(half, half), :].astype(F32)).astype(BF16)
         send(b2.at[zi], bc.at[zi], xsend.at[5, zi], xrecv.at[5, zi], at(xx=xm))
@@ -157,14 +176,15 @@
         zs[dz - 1, half:body] = lower.astype(BF16)
         send(zs.at[dz - 1], zr.at[dz - 1], zsend.at[dz - 1], zrecv.at[dz - 1], at(zz=zi))
 
-    loop(0, NX, lambda n: (pl.when(n == 0)(lambda: landed(cv.at[:, 0], csem.at[0])), tile_sums(n)))
-
+    def far(i):
+        landed(cv.at[:, 0], csem.at[i])
+        tile_sums(xo, (z + order(i)) % NZ)
+
+    loop(0, NZ, far)
     pl.semaphore_wait(barrier, NX - 1 + NZ - 1 + nf - 1)
-    first(0)
+    loop(0, NZ, first)
     for i in range(NX - 1):
         send(degp.at[(x + 1 + i) % NX], dgot.at[i], dsem.at[0, i], dsem.at[1, i], at(xx=(x + 1 + i) % NX))
-    direct_up(0)
-    direct_down(0)
 
     wall[f] = weights[...]
     r2[f, 0:8] = near[f]
@@ -176,33 +196,27 @@
 
     loop(0, nf - 1, early)
 
+    lag = 3
+
     def step(n):
-        i, q = n // NX, n % NX
+        i, q = n // 3, n % 3
+        tile_sums((x + 1 + 2 * q + 3 * (q // 2)) % NX, (z + order(i)) % NZ)
 
         @pl.when(q == 0)
         def _():
-            landed(cv.at[:, 0], csem.at[i])
-
-        tile_sums(n)
-
-        @pl.when(q == 0)
-        def _():
-            first(i)
+            direct_up(i)
+            relay_up(i)
 
         @pl.when(q == 1)
         def _():
-            direct_up(i)
-            relay(i - 1)
-
-        @pl.when((q == 2) & (i >= 2))
+            direct_down(i)
+            relay_down(i)
+
+        @pl.when((q == 2) & (i >= lag))
         def _():
-            onward(i - 2)
-
-        @pl.when(q == 3)
-        def _():
-            direct_down(i)
-
-        @pl.when(n == NX + 3)
+            onward(i - lag)
+
+        @pl.when(n == 7)
         def _():
             for j in range(NX - 1):
                 landed(dgot.at[j], dsem.at[1, j])
@@ -210,15 +224,14 @@
             for dz in range(1, NZ):
                 send(degx, dz_got.at[dz - 1], esem.at[0, dz - 1], esem.at[1, dz - 1], at(zz=(z + dz) % NZ))
 
-    loop(NX, NX * NZ, step)
-    relay(NZ - 1)
-    onward(NZ - 2)
+    loop(0, 3 * NZ, step)
+    loop(NZ - lag, NZ - 1, onward)
 
     own_nodes = lax.broadcasted_iota(jnp.int32, (LANES, nbrs.shape[1]), 0) + f * LANES
     counts = jnp.zeros(own_nodes.shape, F32)
     for n in range(FAN2):
         counts += jnp.where(nbrs[n : n + 1, :] == own_nodes, 1.0, 0.0)
-    counts = counts.astype(BF16)
+    counts = jnp.transpose(counts).astype(BF16)
     deg = degx[pl.ds(z, 1), :]
     for i in range(NZ - 1):
         landed(dz_got.at[i], esem.at[1, i])
@@ -254,7 +267,7 @@
     w1 = wall[:, 0:16, :].reshape(nf * 16, wall.shape[2])
     pre = lax.dot_general(both, w1, (((0,), (0,)), ((), ())), preferred_element_type=F32)
     hidden = jnp.maximum(pre, 0.0).astype(BF16)
-    seed_sums = lax.dot_general(counts, hidden, (((0,), (0,)), ((), ())), preferred_element_type=F32)
+    seed_sums = jnp.dot(counts, hidden, preferred_element_type=F32)
     for p in range(nf):
         piece = seed_sums[p * 8 : p * 8 + 8]
         s3[p] = jnp.concatenate([piece[:, 0:LANES], piece[:, LANES:]], axis=0).astype(BF16)

time: 66.2 us -> 60.9 us (0.920)
  Pallas kernels: 65.4 us -> 60.1 us
    pallas_call x1, Pallas kernels: 61.4 us -> 56.1 us  [seed_logits(): pl.pallas_call(step_kernel, out_shape=jax.ShapeDtypeStruct((feats, seeds...]
where the time goes in v3:
time: 60.9 us; the launch traced here: 60.7 us
  Pallas kernels  60.1 us (99%)
  between operations  0.64 us (1%)
    pallas_call x1, Pallas kernels, seed_logits(): pl.pallas_call(step_kernel, out_shape=jax.ShapeDtypeStruct((feats, seeds...  56.1 us
    pallas_call x1, Pallas kernels, tile_plan(): pl.pallas_call(plan_kernel, out_shape=(ints, ints, jax.ShapeDtypeStruct((...  2.35 us
    pallas_call x1, Pallas kernels, per_device(): pl.pallas_call(loss_kernel, out_shape=(jax.ShapeDtypeStruct((classes, see...  1.65 us

profile of v3, /device:TPU:1, one launch (start us, length us, event | category | flops | bytes accessed | tf_op | source)
XLA Modules:
  0.0 60.7 jit_solution(16516058668234624331)
XLA Ops:
  0.6 2.4 %shard_map.131 = (s32[8,128]{1,0:T(8,128)}, s32[8,128]{1,0:T(8,128)}, f32[4,8,128]{2,1,0:T(8,128)}) custom-call(s32[8,128]{1,0:T(8,128)} %bitcast.23, s32[8,128]{1,0:T(8,128)} %bitcast.15), custom_call_target="tpu_custom_call" | custom-call | tf_op jit(solution)/shard_map/pallas_call | solution.py:363
  3.0 56.1 %shard_map.132 = f32[16,8,256]{2,1,0:T(8,128)} custom-call(s32[1024]{0:T(1024)} %src.1, s32[1024]{0:T(1024)} %rows.1, s32[1024]{0:T(1024)} %bitcast.21, s32[1024]{0:T(1024)} %bitcast.22, bf16[8,16384]{1,0:T(8,128)(2,1)} %x_ref.1, s32[4,8,32,4,128]{4,3,2,1,0:T(4,128)} %bitcast.13, f32[4,8,128]{2,1,0:T(8,128)} %get-tuple-element.9.degp, ...), custom_call_target="tpu_custom_call" | custom-call | tf_op jit(solution)/shard_map/pallas_call | solution.py:381
  59.1 1.6 %shard_map.133 = (f32[172,128]{1,0:T(8,128)}, f32[1,128]{1,0:T(1,128)}) custom-call(f32[128,256]{1,0:T(8,128)} %bitcast.14, s32[1,128]{1,0:T(1,128)} %bitcast.24), custom_call_target="tpu_custom_call" | custom-call | tf_op jit(solution)/shard_map/pallas_call | solution.py:463

commit v4 on v3

--- a/solution.py
+++ b/solution.py
@@ -15,36 +15,35 @@
 F32, BF16 = jnp.float32, jnp.bfloat16
 
 
-def plan_kernel(dst, rows, prev, last, degp):
+def slot_plan(d):
     slots = 32
-    d = dst[...]
-    lane = lax.broadcasted_iota(jnp.int32, d.shape, 1)
-    pos = lane % slots
-    found = jnp.full(d.shape, slots, jnp.int32)
+    pos = lax.broadcasted_iota(jnp.int32, d.shape, 1) % slots
+    prev = jnp.full(d.shape, slots, jnp.int32)
     for s in range(slots - 1, 0, -1):
-        found = jnp.where((pos >= s) & (pltpu.roll(d, s, 1) == d), pos - s, found)
-    prev[...] = found
-    ends = jnp.full(d.shape, slots, jnp.int32)
+        prev = jnp.where((pos >= s) & (pltpu.roll(d, s, 1) == d), pos - s, prev)
+    last = jnp.full(d.shape, slots, jnp.int32)
     for b in range(16):
         v = jnp.where(d == b, pos, -1)
         for s in (1, 2, 4, 8, 16):
             v = jnp.maximum(v, jnp.where((pos & s) == 0, pltpu.roll(v, LANES - s, 1), pltpu.roll(v, s, 1)))
-        ends = jnp.where((pos == b) & (v >= 0), v, ends)
-    last[...] = ends
-    mine = jnp.where(d == lax.axis_index("feat"), rows[...], 0).astype(F32)
-    columns = jnp.transpose(jnp.concatenate([mine] * 16, axis=0))
+        last = jnp.where((pos == b) & (v >= 0), v, last)
+    return prev, last
+
+
+def block_counts(rows, degp):
+    columns = jnp.transpose(jnp.concatenate([rows.astype(F32)] * 16, axis=0))
     across = lax.broadcasted_iota(jnp.int32, (LANES, LANES), 1).astype(F32)
     for r in range(8):
         live = jnp.where(across < columns[:, r : r + 1], 1.0, 0.0)
-        sums = jnp.sum(live.reshape(4, slots, LANES), axis=1)
+        sums = jnp.sum(live.reshape(4, LANES // 4, LANES), axis=1)
         degp[r // 2, (r % 2) * 4 : (r % 2) * 4 + 4, :] = sums
 
 
 def step_kernel(
-    src, rows, prev, last, x_ref, cols, degp, xnear, self1, neigh1, self2, neigh2, nbrs, out,
-    xs, cv, buf, parts, stage, weights, wall, a1, b1, a2, b2, ac, ao, bo, bc, dgot, degx, dz_got,
+    src, rows, dst_v, rows_v, x_ref, cols, xnear, self1, neigh1, self2, neigh2, nbrs, out,
+    plan_v, plan_s, degp, xs, cv, buf, parts, stage, weights, wall, a1, b1, a2, b2, ac, ao, bo, bc, dgot, degx, dz_got,
     zs, zr, near, sums, r2, s3, hs, r3, rh, s4, r4,
-    csem, wsem, nsem, xsend, xrecv, dsem, esem, zsend, zrecv, fsem, gsend, grecv, psem,
+    plan_sem, csem, wsem, nsem, xsend, xrecv, dsem, esem, zsend, zrecv, fsem, gsend, grecv, psem,
 ):
     node, f = lax.axis_index("node"), lax.axis_index("feat")
     x, z = node // NZ, node % NZ
@@ -89,6 +88,11 @@
 
     loop(0, NZ, columns_in)
 
+    targets = dst_v[...]
+    plan_v[0:8], plan_v[8:16] = slot_plan(targets)
+    plan_copy = pltpu.make_async_copy(plan_v, plan_s, plan_sem)
+    plan_copy.start()
+    block_counts(jnp.where(targets == f, rows_v[...], 0), degp)
     for b in range(xs.shape[0]):
         xs[b] = x_ref[:, b * LANES : (b + 1) * LANES].astype(F32)
     buf[...] = jnp.zeros_like(buf)
@@ -126,13 +130,14 @@
         return jnp.dot(block.astype(BF16), matrix, preferred_element_type=F32)
 
     def tile_sums(xx, zi):
-        base = (xx * NZ + zi) * slots
+        target = xx * NZ + zi
+        base, line, lane0 = target * slots, target // 4, target % 4 * slots
         for s in range(slots):
             block = xs[src[base + s]]
-            total = (counted if s % 2 else gathered)(block, xx, zi, s)
-            buf[s] = jnp.where(lane < rows[base + s], total, 0.0) + buf[prev[base + s]]
+            total = (counted if s % 8 in (2, 5, 7) else gathered)(block, xx, zi, s)
+            buf[s] = jnp.where(lane < rows[base + s], total, 0.0) + buf[plan_s[line, lane0 + s]]
         for b in range(0, nf, 2):
-            pair = [buf[last[base + b]], buf[last[base + b + 1]]]
+            pair = [buf[plan_s[8 + line, lane0 + b + j]] for j in (0, 1)]
             parts[xx, zi, b * 8 : b * 8 + 16] = jnp.concatenate(pair, axis=0).astype(BF16)
 
     def first(i):
@@ -175,6 +180,8 @@
         zs[dz - 1, 0:half] = upper.astype(BF16)
         zs[dz - 1, half:body] = lower.astype(BF16)
         send(zs.at[dz - 1], zr.at[dz - 1], zsend.at[dz - 1], zrecv.at[dz - 1], at(zz=zi))
+
+    plan_copy.wait()
 
     def far(i):
         landed(cv.at[:, 0], csem.at[i])
@@ -357,17 +364,7 @@
         out[i] = r4[i % 2, i // 2]
 
 
-def tile_plan(dst, rows):
-    shape = (8, LANES)
-    ints = jax.ShapeDtypeStruct(shape, jnp.int32)
-    return pl.pallas_call(
-        plan_kernel,
-        out_shape=(ints, ints, jax.ShapeDtypeStruct((NX, NZ, LANES), F32)),
-        compiler_params=pltpu.CompilerParams(vmem_limit_bytes=VMEM),
-    )(dst.reshape(shape), rows.reshape(shape))
-
-
-def seed_logits(src, rows, x, cols, degp, prev, last, xnear, w, nbrs, feats):
+def seed_logits(src, dst, rows, x, cols, xnear, w, nbrs, feats):
     self1, neigh1, self2, neigh2 = w
     hid = self1.shape[1]
     seeds = nbrs.shape[1]
@@ -381,9 +378,12 @@
     return pl.pallas_call(
         step_kernel,
         out_shape=jax.ShapeDtypeStruct((feats, seeds // feats, hid), F32),
-        in_specs=[sm] * 4 + [vm, pl.BlockSpec(memory_space=pl.ANY)] + [vm] * 7,
+        in_specs=[sm] * 2 + [vm] * 3 + [pl.BlockSpec(memory_space=pl.ANY)] + [vm] * 6,
         out_specs=vm,
         scratch_shapes=[
+            pltpu.VMEM((16, LANES), jnp.int32),
+            pltpu.SMEM((16, LANES), jnp.int32),
+            pltpu.VMEM((NX, NZ, LANES), F32),
             pltpu.VMEM((x.shape[1] // LANES, 8, LANES), F32),
             pltpu.VMEM((NX, NZ, slots, depth, LANES), jnp.int32),
             pltpu.VMEM((slots + 1, 8, LANES), F32),
@@ -406,6 +406,7 @@
             pltpu.VMEM((16, LANES), BF16),
             pltpu.VMEM((8, hid), F32),
             pltpu.VMEM((2, feats // 2, 8, hid), F32),
+            dma(()),
             dma((NZ,)),
             dma((2,)),
             dma((2, feats)),
@@ -424,8 +425,8 @@
             collective_id=0, has_side_effects=True, vmem_limit_bytes=VMEM
         ),
     )(
-        src, rows, prev.reshape(-1), last.reshape(-1), x, cols.reshape(NX, NZ, slots, depth, LANES),
-        degp, xnear, self1, neigh1, self2, neigh2, nbrs,
+        src, rows, dst.reshape(8, LANES), rows.reshape(8, LANES), x,
+        cols.reshape(NX, NZ, slots, depth, LANES), xnear, self1, neigh1, self2, neigh2, nbrs,
     )
 
 
@@ -455,10 +456,9 @@
     feats = lax.axis_size("feat")
     classes, hid = self_two.shape[0], self_one.shape[0]
     seeds = labels.shape[0]
-    prev, last, degp = tile_plan(tile_dst, tile_rows)
     weights = (self_one.T, neigh_one.T, self_two.T, neigh_two.T)
     table = seed_logits(
-        tile_src, tile_rows, x_far, tile_cols, degp, prev, last, x_near, weights, seed_nbrs.T, feats
+        tile_src, tile_dst, tile_rows, x_far, tile_cols, x_near, weights, seed_nbrs.T, feats
     )
     logits, loss = pl.pallas_call(
         loss_kernel,

time: 60.9 us -> 58.2 us (0.956)
  Pallas kernels: 60.1 us -> 57.4 us
    pallas_call x1 -> x0, Pallas kernels: 2.35 us -> none  [tile_plan(): pl.pallas_call(plan_kernel, out_shape=(ints, ints, jax.ShapeDtypeStruct((...]
where the time goes in v4:
time: 58.2 us; the launch traced here: 58.1 us
  Pallas kernels  57.4 us (99%)
  between operations  0.64 us (1%)
    pallas_call x1, Pallas kernels, seed_logits(): pl.pallas_call(step_kernel, out_shape=jax.ShapeDtypeStruct((feats, seeds...  55.8 us
    pallas_call x1, Pallas kernels, per_device(): pl.pallas_call(loss_kernel, out_shape=(jax.ShapeDtypeStruct((classes, see...  1.65 us

profile of v4, /device:TPU:1, one launch (start us, length us, event | category | flops | bytes accessed | tf_op | source)
XLA Modules:
  0.0 58.1 jit_solution(7353520099174274210)
XLA Ops:
  0.6 55.8 %shard_map.131 = f32[16,8,256]{2,1,0:T(8,128)} custom-call(s32[1024]{0:T(1024)} %src.1, s32[1024]{0:T(1024)} %rows.1, s32[8,128]{1,0:T(8,128)} %bitcast.17, s32[8,128]{1,0:T(8,128)} %bitcast.13, bf16[8,16384]{1,0:T(8,128)(2,1)} %x_ref.1, s32[4,8,32,4,128]{4,3,2,1,0:T(4,128)} %bitcast.11, bf16[8,2048]{1,0:T(8,128)(2,1)} %xnear.1, bf16[8,256]{1,0:T(8,128)(2,1)} %bitcast.18, ...), custom_call_target="tpu_custom_call" | custom-call | tf_op jit(solution)/shard_map/pallas_call | solution.py:378
  56.4 1.6 %shard_map.132 = (f32[172,128]{1,0:T(8,128)}, f32[1,128]{1,0:T(1,128)}) custom-call(f32[128,256]{1,0:T(8,128)} %bitcast.12, s32[1,128]{1,0:T(1,128)} %bitcast.20), custom_call_target="tpu_custom_call" | custom-call | tf_op jit(solution)/shard_map/pallas_call | solution.py:463

commit v5 on v4

--- a/solution.py
+++ b/solution.py
@@ -42,7 +42,7 @@
 def step_kernel(
     src, rows, dst_v, rows_v, x_ref, cols, xnear, self1, neigh1, self2, neigh2, nbrs, out,
     plan_v, plan_s, degp, xs, cv, buf, parts, stage, weights, wall, a1, b1, a2, b2, ac, ao, bo, bc, dgot, degx, dz_got,
-    zs, zr, near, sums, r2, s3, hs, r3, rh, s4, r4,
+    zs, zr, picks, w1t, near, sums, r2, s3, hs, r3, rh, s4, r4,
     plan_sem, csem, wsem, nsem, xsend, xrecv, dsem, esem, zsend, zrecv, fsem, gsend, grecv, psem,
 ):
     node, f = lax.axis_index("node"), lax.axis_index("feat")
@@ -88,11 +88,9 @@
 
     loop(0, NZ, columns_in)
 
-    targets = dst_v[...]
-    plan_v[0:8], plan_v[8:16] = slot_plan(targets)
+    plan_v[0:8], plan_v[8:16] = slot_plan(dst_v[...])
     plan_copy = pltpu.make_async_copy(plan_v, plan_s, plan_sem)
     plan_copy.start()
-    block_counts(jnp.where(targets == f, rows_v[...], 0), degp)
     for b in range(xs.shape[0]):
         xs[b] = x_ref[:, b * LANES : (b + 1) * LANES].astype(F32)
     buf[...] = jnp.zeros_like(buf)
@@ -183,67 +181,66 @@
 
     plan_copy.wait()
 
-    def far(i):
+    def own_x(i):
         landed(cv.at[:, 0], csem.at[i])
-        tile_sums(xo, (z + order(i)) % NZ)
-
-    loop(0, NZ, far)
-    pl.semaphore_wait(barrier, NX - 1 + NZ - 1 + nf - 1)
-    loop(0, NZ, first)
-    for i in range(NX - 1):
-        send(degp.at[(x + 1 + i) % NX], dgot.at[i], dsem.at[0, i], dsem.at[1, i], at(xx=(x + 1 + i) % NX))
-
+        tile_sums(x, (z + order(i)) % NZ)
+
+    loop(0, NZ, own_x)
     wall[f] = weights[...]
     r2[f, 0:8] = near[f]
+    pl.semaphore_wait(barrier, NX - 1 + NZ - 1 + nf - 1)
 
     def early(i):
         p = (f + 1 + i) % nf
         send(near.at[p], r2.at[f, pl.ds(0, 8)], nsem.at[0, 0], nsem.at[1, f], at(ff=p))
         send(weights, wall.at[f], wsem.at[0], wsem.at[1], at(ff=p))
 
-    loop(0, nf - 1, early)
-
-    lag = 3
-
-    def step(n):
-        i, q = n // 3, n % 3
-        tile_sums((x + 1 + 2 * q + 3 * (q // 2)) % NX, (z + order(i)) % NZ)
-
-        @pl.when(q == 0)
+    def far(i):
+        early(i)
+        tile_sums(xo, (z + order(i)) % NZ)
+        first(i)
+
+    loop(0, NZ, far)
+    onward_lag = 4
+
+    def beside(i):
+        zi = (z + order(i)) % NZ
+
+        @pl.when(i < nf - 1 - NZ)
         def _():
-            direct_up(i)
-            relay_up(i)
-
-        @pl.when(q == 1)
+            early(NZ + i)
+
+        tile_sums(xp, zi)
+        direct_up(i)
+        relay_up(i)
+        tile_sums(xm, zi)
+        direct_down(i)
+        relay_down(i)
+
+        @pl.when(i >= onward_lag)
         def _():
-            direct_down(i)
-            relay_down(i)
-
-        @pl.when((q == 2) & (i >= lag))
-        def _():
-            onward(i - lag)
-
-        @pl.when(n == 7)
-        def _():
-            for j in range(NX - 1):
-                landed(dgot.at[j], dsem.at[1, j])
-            degx[...] = degp[x] + dgot[0] + dgot[1] + dgot[2]
-            for dz in range(1, NZ):
-                send(degx, dz_got.at[dz - 1], esem.at[0, dz - 1], esem.at[1, dz - 1], at(zz=(z + dz) % NZ))
-
-    loop(0, 3 * NZ, step)
-    loop(NZ - lag, NZ - 1, onward)
+            onward(i - onward_lag)
+
+    loop(0, NZ, beside)
+
+    block_counts(jnp.where(dst_v[...] == f, rows_v[...], 0), degp)
+    for i in range(NX - 1):
+        send(degp.at[(x + 1 + i) % NX], dgot.at[i], dsem.at[0, i], dsem.at[1, i], at(xx=(x + 1 + i) % NX))
+    loop(NZ - onward_lag, NZ - 1, onward)
+    for i in range(NX - 1):
+        landed(dgot.at[i], dsem.at[1, i])
+    degx[...] = degp[x] + dgot[0] + dgot[1] + dgot[2]
+    for dz in range(1, NZ):
+        send(degx, dz_got.at[dz - 1], esem.at[0, dz - 1], esem.at[1, dz - 1], at(zz=(z + dz) % NZ))
 
     own_nodes = lax.broadcasted_iota(jnp.int32, (LANES, nbrs.shape[1]), 0) + f * LANES
     counts = jnp.zeros(own_nodes.shape, F32)
     for n in range(FAN2):
         counts += jnp.where(nbrs[n : n + 1, :] == own_nodes, 1.0, 0.0)
-    counts = jnp.transpose(counts).astype(BF16)
-    deg = degx[pl.ds(z, 1), :]
-    for i in range(NZ - 1):
-        landed(dz_got.at[i], esem.at[1, i])
-        deg += dz_got[i, pl.ds(z, 1), :]
-    deg = jnp.maximum(4.0 * deg, 1.0)
+    picks[...] = jnp.transpose(counts).astype(BF16)
+    landed(wall.at[pl.ds(0, nf - 1)], wsem.at[1])
+    w1 = wall[:, 0:16, :].reshape(nf * 16, wall.shape[2])
+    w1t[...] = jnp.transpose(w1.astype(F32)).astype(BF16)
 
     upper, lower = summed(NZ - 1)
     for i in (3, 2, 4, 1, 5, 0, 6):
@@ -260,7 +257,11 @@
 
     loop(0, nf - 1, spread)
     r2[f, 8:16] = sums[f]
-    landed(wall.at[pl.ds(0, nf - 1)], wsem.at[1])
+    deg = degx[pl.ds(z, 1), :]
+    for i in range(NZ - 1):
+        landed(dz_got.at[i], esem.at[1, i])
+        deg += dz_got[i, pl.ds(z, 1), :]
+    scale = 1.0 / jnp.maximum(4.0 * deg, 1.0)
 
     def near_in(i):
         p = (f + 1 + i) % nf
@@ -270,18 +271,22 @@
     landed(sums.at[pl.ds(0, nf - 1)], fsem.at[1])
     both = r2[...].reshape(nf * 16, LANES)
     is_sum = lax.broadcasted_iota(jnp.int32, both.shape, 0) % 16 >= 8
-    both = jnp.where(is_sum, both / deg, both).astype(BF16)
-    w1 = wall[:, 0:16, :].reshape(nf * 16, wall.shape[2])
-    pre = lax.dot_general(both, w1, (((0,), (0,)), ((), ())), preferred_element_type=F32)
-    hidden = jnp.maximum(pre, 0.0).astype(BF16)
-    seed_sums = jnp.dot(counts, hidden, preferred_element_type=F32)
+    both = jnp.where(is_sum, both * scale, both).astype(BF16)
+    hidden = jnp.maximum(jnp.dot(w1t[...], both, preferred_element_type=F32), 0.0).astype(BF16)
+    across = (((1,), (1,)), ((), ()))
+    seed_sums = lax.dot_general(picks[...], hidden, across, preferred_element_type=F32)
     for p in range(nf):
         piece = seed_sums[p * 8 : p * 8 + 8]
         s3[p] = jnp.concatenate([piece[:, 0:LANES], piece[:, LANES:]], axis=0).astype(BF16)
 
     @pl.when(f == 0)
     def _():
-        wide = hidden.astype(F32)
+        diagonal = lax.broadcasted_iota(jnp.int32, (LANES, LANES), 0) == lax.broadcasted_iota(
+            jnp.int32, (LANES, LANES), 1
+        )
+        wide = lax.dot_general(
+            jnp.where(diagonal, 1.0, 0.0).astype(BF16), hidden, across, preferred_element_type=F32
+        )
         for p in range(nf):
             piece = wide[p * 8 : p * 8 + 8]
             hs[p] = jnp.concatenate([piece[:, 0:LANES], piece[:, LANES:]], axis=0).astype(BF16)
@@ -329,12 +334,12 @@
     send(s4, r4.at[core, y], gsend.at[nf // 2 - 1], psem.at[1, y], other)
     r4[core, y] = logits
 
-    def across(i):
+    def onto(i):
         yy = (y + nf + (1 - 2 * (i % 2)) * (i // 2 + 1)) % (nf // 2)
         landed(s4, grecv.at[yy])
         send(r4.at[core, yy], r4.at[core, yy], psem.at[0, i], psem.at[1, yy], other)
 
-    loop(0, nf // 2 - 1, across)
+    loop(0, nf // 2 - 1, onto)
 
     def sent(i):
         for kind, ref in ((0, a1), (1, b1), (2, bo), (3, ao), (4, ac), (5, bc)):
@@ -397,6 +402,8 @@
             pltpu.VMEM((NZ - 1, NZ, LANES), F32),
             pltpu.VMEM((NZ - 1, body, LANES), BF16),
             pltpu.VMEM((NZ - 1, body, LANES), BF16),
+            pltpu.VMEM((seeds, LANES), BF16),
+            pltpu.VMEM((hid, feats * 16), BF16),
             pltpu.VMEM((feats, 8, LANES), F32),
             pltpu.VMEM((feats, 8, LANES), F32),
             pltpu.VMEM((feats, 16, LANES), F32),

time: 58.2 us -> 56.4 us (0.969)
  Pallas kernels: 57.4 us -> 55.6 us
    pallas_call x1, Pallas kernels: 55.8 us -> 53.9 us  [seed_logits(): pl.pallas_call(step_kernel, out_shape=jax.ShapeDtypeStruct((feats, seeds...]
where the time goes in v5:
time: 56.4 us; the launch traced here: 56.2 us
  Pallas kernels  55.6 us (99%)
  between operations  0.64 us (1%)
    pallas_call x1, Pallas kernels, seed_logits(): pl.pallas_call(step_kernel, out_shape=jax.ShapeDtypeStruct((feats, seeds...  53.9 us
    pallas_call x1, Pallas kernels, per_device(): pl.pallas_call(loss_kernel, out_shape=(jax.ShapeDtypeStruct((classes, see...  1.65 us

profile of v5, /device:TPU:1, one launch (start us, length us, event | category | flops | bytes accessed | tf_op | source)
XLA Modules:
  0.0 56.2 jit_solution(12603764107398400919)
XLA Ops:
  0.6 53.9 %shard_map.131 = f32[16,8,256]{2,1,0:T(8,128)} custom-call(s32[1024]{0:T(1024)} %src.1, s32[1024]{0:T(1024)} %rows.1, s32[8,128]{1,0:T(8,128)} %bitcast.17, s32[8,128]{1,0:T(8,128)} %bitcast.13, bf16[8,16384]{1,0:T(8,128)(2,1)} %x_ref.1, s32[4,8,32,4,128]{4,3,2,1,0:T(4,128)} %bitcast.11, bf16[8,2048]{1,0:T(8,128)(2,1)} %xnear.1, bf16[8,256]{1,0:T(8,128)(2,1)} %bitcast.18, ...), custom_call_target="tpu_custom_call" | custom-call | tf_op jit(solution)/shard_map/pallas_call | solution.py:383
  54.6 1.6 %shard_map.132 = (f32[172,128]{1,0:T(8,128)}, f32[1,128]{1,0:T(1,128)}) custom-call(f32[128,256]{1,0:T(8,128)} %bitcast.12, s32[1,128]{1,0:T(1,128)} %bitcast.20), custom_call_target="tpu_custom_call" | custom-call | tf_op jit(solution)/shard_map/pallas_call | solution.py:470

commit v6 on v5

--- a/solution.py
+++ b/solution.py
@@ -69,6 +69,9 @@
 
     def order(i):
         return (4 + (1 - 2 * (i % 2)) * ((i + 1) // 2)) % NZ
+
+    def peer(i):
+        return (f + nf // 2 + (1 - 2 * (i % 2)) * ((i + 1) // 2)) % nf
 
     def loop(lo, hi, fn):
         lax.fori_loop(lo, hi, lambda i, c: (fn(i), c)[1], 0)
@@ -181,41 +184,45 @@
 
     plan_copy.wait()
 
-    def own_x(i):
-        landed(cv.at[:, 0], csem.at[i])
-        tile_sums(x, (z + order(i)) % NZ)
-
-    loop(0, NZ, own_x)
     wall[f] = weights[...]
     r2[f, 0:8] = near[f]
-    pl.semaphore_wait(barrier, NX - 1 + NZ - 1 + nf - 1)
 
     def early(i):
-        p = (f + 1 + i) % nf
+        p = peer(i)
         send(near.at[p], r2.at[f, pl.ds(0, 8)], nsem.at[0, 0], nsem.at[1, f], at(ff=p))
         send(weights, wall.at[f], wsem.at[0], wsem.at[1], at(ff=p))
 
     def far(i):
+        landed(cv.at[:, 0], csem.at[i])
+        tile_sums(xo, (z + order(i)) % NZ)
+
+    ahead = 1
+    loop(0, ahead, far)
+    pl.semaphore_wait(barrier, NX - 1 + NZ - 1 + nf - 1)
+    loop(0, ahead, first)
+
+    def far_out(i):
+        far(i)
+        first(i)
+
+    loop(ahead, NZ, far_out)
+    onward_lag = 3
+
+    def beside(i):
+        zi = (z + order(i)) % NZ
         early(i)
-        tile_sums(xo, (z + order(i)) % NZ)
-        first(i)
-
-    loop(0, NZ, far)
-    onward_lag = 4
-
-    def beside(i):
-        zi = (z + order(i)) % NZ
-
-        @pl.when(i < nf - 1 - NZ)
-        def _():
-            early(NZ + i)
-
         tile_sums(xp, zi)
         direct_up(i)
         relay_up(i)
         tile_sums(xm, zi)
         direct_down(i)
         relay_down(i)
+
+        @pl.when(i < nf - 1 - NZ)
+        def _():
+            early(NZ + i)
+
+        tile_sums(x, zi)
 
         @pl.when(i >= onward_lag)
         def _():
@@ -252,7 +259,7 @@
         sums[b + nf // 2] = lower[b * 8 : b * 8 + 8]
 
     def spread(i):
-        p = (f + 1 + i) % nf
+        p = peer(i)
         send(sums.at[p], r2.at[f, pl.ds(8, 8)], fsem.at[0], fsem.at[1], at(ff=p))
 
     loop(0, nf - 1, spread)
@@ -292,7 +299,7 @@
             hs[p] = jnp.concatenate([piece[:, 0:LANES], piece[:, LANES:]], axis=0).astype(BF16)
 
     def seeds_out(i):
-        p = (f + 1 + i) % nf
+        p = peer(i)
         send(s3.at[p], r3.at[f], fsem.at[2], fsem.at[3], at(ff=p))
 
         @pl.when(f == 0)
@@ -327,7 +334,7 @@
     other = at(ff=f + 1 - 2 * core)
 
     def along(i):
-        yy = (y + 1 + i) % (nf // 2)
+        yy = (y + order(i)) % (nf // 2)
         send(s4, r4.at[core, y], gsend.at[i], grecv.at[y], at(ff=yy * 2 + core))
 
     loop(0, nf // 2 - 1, along)

time: 56.4 us -> 53.2 us (0.943)
  Pallas kernels: 55.6 us -> 52.4 us
    pallas_call x1, Pallas kernels: 53.9 us -> 50.8 us  [seed_logits(): pl.pallas_call(step_kernel, out_shape=jax.ShapeDtypeStruct((feats, seeds...]
where the time goes in v6:
time: 53.2 us; the launch traced here: 53.1 us
  Pallas kernels  52.4 us (98%)
  between operations  0.64 us (1%)
    pallas_call x1, Pallas kernels, seed_logits(): pl.pallas_call(step_kernel, out_shape=jax.ShapeDtypeStruct((feats, seeds...  50.8 us
    pallas_call x1, Pallas kernels, per_device(): pl.pallas_call(loss_kernel, out_shape=(jax.ShapeDtypeStruct((classes, see...  1.65 us

profile of v6, /device:TPU:1, one launch (start us, length us, event | category | flops | bytes accessed | tf_op | source)
XLA Modules:
  0.0 53.1 jit_solution(17823134989607723729)
XLA Ops:
  0.6 50.8 %shard_map.131 = f32[16,8,256]{2,1,0:T(8,128)} custom-call(s32[1024]{0:T(1024)} %src.1, s32[1024]{0:T(1024)} %rows.1, s32[8,128]{1,0:T(8,128)} %bitcast.17, s32[8,128]{1,0:T(8,128)} %bitcast.13, bf16[8,16384]{1,0:T(8,128)(2,1)} %x_ref.1, s32[4,8,32,4,128]{4,3,2,1,0:T(4,128)} %bitcast.11, bf16[8,2048]{1,0:T(8,128)(2,1)} %xnear.1, bf16[8,256]{1,0:T(8,128)(2,1)} %bitcast.18, ...), custom_call_target="tpu_custom_call" | custom-call | tf_op jit(solution)/shard_map/pallas_call | solution.py:390
  51.4 1.6 %shard_map.132 = (f32[172,128]{1,0:T(8,128)}, f32[1,128]{1,0:T(1,128)}) custom-call(f32[128,256]{1,0:T(8,128)} %bitcast.12, s32[1,128]{1,0:T(1,128)} %bitcast.20), custom_call_target="tpu_custom_call" | custom-call | tf_op jit(solution)/shard_map/pallas_call | solution.py:477

commit v7 on v6

--- a/solution.py
+++ b/solution.py
@@ -41,7 +41,7 @@
 
 def step_kernel(
     src, rows, dst_v, rows_v, x_ref, cols, xnear, self1, neigh1, self2, neigh2, nbrs, out,
-    plan_v, plan_s, degp, xs, cv, buf, parts, stage, weights, wall, a1, b1, a2, b2, ac, ao, bo, bc, dgot, degx, dz_got,
+    plan_v, plan_s, degp, xs, cv, buf0, buf1, buf2, parts, stage, weights, wall, a1, b1, a2, b2, ac, ao, bo, bc, dgot, degx, dz_got,
     zs, zr, picks, w1t, near, sums, r2, s3, hs, r3, rh, s4, r4,
     plan_sem, csem, wsem, nsem, xsend, xrecv, dsem, esem, zsend, zrecv, fsem, gsend, grecv, psem,
 ):
@@ -96,7 +96,8 @@
     plan_copy.start()
     for b in range(xs.shape[0]):
         xs[b] = x_ref[:, b * LANES : (b + 1) * LANES].astype(F32)
-    buf[...] = jnp.zeros_like(buf)
+    for buf in (buf0, buf1, buf2):
+        buf[...] = jnp.zeros_like(buf)
     for b in range(nf):
         near[b] = xnear[:, b * LANES : (b + 1) * LANES].astype(F32)
     stage[...] = jnp.zeros_like(stage)
@@ -130,7 +131,7 @@
         matrix = jnp.concatenate(groups, axis=0)
         return jnp.dot(block.astype(BF16), matrix, preferred_element_type=F32)
 
-    def tile_sums(xx, zi):
+    def tile_sums(xx, zi, buf):
         target = xx * NZ + zi
         base, line, lane0 = target * slots, target // 4, target % 4 * slots
         for s in range(slots):
@@ -192,37 +193,37 @@
         send(near.at[p], r2.at[f, pl.ds(0, 8)], nsem.at[0, 0], nsem.at[1, f], at(ff=p))
         send(weights, wall.at[f], wsem.at[0], wsem.at[1], at(ff=p))
 
-    def far(i):
-        landed(cv.at[:, 0], csem.at[i])
-        tile_sums(xo, (z + order(i)) % NZ)
-
-    ahead = 1
-    loop(0, ahead, far)
+    def far(j):
+        for i in (2 * j, 2 * j + 1):
+            landed(cv.at[:, 0], csem.at[i])
+        tile_sums(xo, (z + order(2 * j)) % NZ, buf0)
+        tile_sums(xo, (z + order(2 * j + 1)) % NZ, buf1)
+
+    def far_out(j):
+        far(j)
+        first(2 * j)
+        first(2 * j + 1)
+
+    far(0)
     pl.semaphore_wait(barrier, NX - 1 + NZ - 1 + nf - 1)
-    loop(0, ahead, first)
-
-    def far_out(i):
-        far(i)
-        first(i)
-
-    loop(ahead, NZ, far_out)
+    loop(0, 2, first)
+    loop(1, NZ // 2, far_out)
     onward_lag = 3
 
     def beside(i):
         zi = (z + order(i)) % NZ
         early(i)
-        tile_sums(xp, zi)
+        tile_sums(xp, zi, buf0)
+        tile_sums(xm, zi, buf1)
         direct_up(i)
+        direct_down(i)
         relay_up(i)
-        tile_sums(xm, zi)
-        direct_down(i)
         relay_down(i)
+        tile_sums(x, zi, buf2)
 
         @pl.when(i < nf - 1 - NZ)
         def _():
             early(NZ + i)
-
-        tile_sums(x, zi)
 
         @pl.when(i >= onward_lag)
         def _():
@@ -398,7 +399,7 @@
             pltpu.VMEM((NX, NZ, LANES), F32),
             pltpu.VMEM((x.shape[1] // LANES, 8, LANES), F32),
             pltpu.VMEM((NX, NZ, slots, depth, LANES), jnp.int32),
-            pltpu.VMEM((slots + 1, 8, LANES), F32),
+            *[pltpu.VMEM((slots + 1, 8, LANES), F32)] * 3,
             pltpu.VMEM((NX, NZ, body, LANES), BF16),
             pltpu.VMEM((48, hid), F32),
             pltpu.VMEM((48, hid), BF16),

time: 53.2 us -> 53.7 us (level)
  no operation moved by 1% of the time
where the time goes in v7:
time: 53.7 us; the launch traced here: 53.5 us
  Pallas kernels  52.9 us (99%)
  between operations  0.64 us (1%)
    pallas_call x1, Pallas kernels, seed_logits(): pl.pallas_call(step_kernel, out_shape=jax.ShapeDtypeStruct((feats, seeds...  51.3 us
    pallas_call x1, Pallas kernels, per_device(): pl.pallas_call(loss_kernel, out_shape=(jax.ShapeDtypeStruct((classes, see...  1.65 us

profile of v7, /device:TPU:1, one launch (start us, length us, event | category | flops | bytes accessed | tf_op | source)
XLA Modules:
  0.0 53.5 jit_solution(11555271253593103649)
XLA Ops:
  0.6 51.3 %shard_map.131 = f32[16,8,256]{2,1,0:T(8,128)} custom-call(s32[1024]{0:T(1024)} %src.1, s32[1024]{0:T(1024)} %rows.1, s32[8,128]{1,0:T(8,128)} %bitcast.17, s32[8,128]{1,0:T(8,128)} %bitcast.13, bf16[8,16384]{1,0:T(8,128)(2,1)} %x_ref.1, s32[4,8,32,4,128]{4,3,2,1,0:T(4,128)} %bitcast.11, bf16[8,2048]{1,0:T(8,128)(2,1)} %xnear.1, bf16[8,256]{1,0:T(8,128)(2,1)} %bitcast.18, ...), custom_call_target="tpu_custom_call" | custom-call | tf_op jit(solution)/shard_map/pallas_call | solution.py:391
  51.9 1.6 %shard_map.132 = (f32[172,128]{1,0:T(8,128)}, f32[1,128]{1,0:T(1,128)}) custom-call(f32[128,256]{1,0:T(8,128)} %bitcast.12, s32[1,128]{1,0:T(1,128)} %bitcast.20), custom_call_target="tpu_custom_call" | custom-call | tf_op jit(solution)/shard_map/pallas_call | solution.py:478
